TPU v7x, 512 devices: a whole 4x8x8 slice. The times are simulated.
512 devices in a mesh: row: 64 (over y_hi, z, core), col: 8 (over x, y_lo).
Axes of the slice: x: 4, y: 8 (y_hi: 4, y_lo: 2; y = y_hi * 2 + y_lo), z: 8, core: 2. Of those that a mesh axis runs over, the one named last changes fastest.
Arguments:
- dens_a: bfloat16 [64, 8, 1, 3, 256, 256], P('row', 'col')
- dens_b: bfloat16 [64, 8, 1, 3, 256, 256], P('row', 'col')
- codes_a: int32 [64, 8, 1, 3], P('row', 'col'), may hold values from 0 to 4, as said below
- codes_b: int32 [64, 8, 1, 3], P('row', 'col'), may hold values from 0 to 4, as said below
- counts_a: int32 [64, 8, 1], P('row', 'col'), may hold values from 1 to 3
- counts_b: int32 [64, 8, 1], P('row', 'col'), may hold values from 1 to 3
Outputs:
- new_a: bfloat16 [64, 8, 1, 3, 256, 256], P('row', 'col')
- new_b: bfloat16 [64, 8, 1, 3, 256, 256], P('row', 'col')
Inputs may be any that keep to these rules, and one draw needn't show every extreme that they name: `codes_a`: within a block row the codes of all slots are distinct. `codes_b`: within a block row the codes of all slots are distinct.
All inputs are finite; a program needn't handle non-finite values.
Results may differ from a plain program's by a relative error of at most 0.0092.
Values may be sent and summed in bfloat16 or wider, within the bound.
A program may use at most 64 MiB of HBM per device.

v0:
```python
import jax
import jax.numpy as jnp
from jax import lax
from jax.sharding import PartitionSpec as P

ITERS = 2


def padded_2(cells, sides, width):
    for axis, dim in sides:
        count = lax.axis_size(axis)
        head = lax.slice_in_dim(cells, 0, width, axis=dim)
        tail = lax.slice_in_dim(cells, cells.shape[dim] - width, cells.shape[dim], axis=dim)
        cells = jnp.concatenate(
            [
                lax.ppermute(tail, axis, [(i, (i + 1) % count) for i in range(count)]),
                cells,
                lax.ppermute(head, axis, [((i + 1) % count, i) for i in range(count)]),
            ],
            axis=dim,
        )
    return cells


def displacement(direction):
    vertical = (direction == 2).astype(jnp.int32) - (direction == 1).astype(jnp.int32)
    lateral = (direction == 4).astype(jnp.int32) - (direction == 3).astype(jnp.int32)
    return (vertical, lateral)


def purify_region(tiles, codes, counts):
    rows = tiles.shape[1]
    slots = tiles.shape[2]
    edge = tiles.shape[3]
    flat_tiles = tiles.reshape(5 * rows, slots, edge, edge)
    flat_codes = codes.reshape(5 * rows, slots)
    flat_counts = counts.reshape(5 * rows)
    own_codes = codes[0]
    order = jnp.arange(slots, dtype=jnp.int32)
    own_live = order[None, :] < counts[0][:, None]
    partner = jnp.take(flat_tiles, own_codes, axis=0)
    partner_codes = jnp.take(flat_codes, own_codes, axis=0)
    partner_live = order[None, None, :] < jnp.take(flat_counts, own_codes, axis=0)[:, :, None]
    first_vert, first_side = displacement(own_codes // rows)
    second_vert, second_side = displacement(partner_codes // rows)
    matches = own_live[:, :, None, None] & partner_live[:, :, :, None] & own_live[:, None, None, :]
    matches = matches & (
        first_vert[:, :, None, None] + second_vert[:, :, :, None] == first_vert[:, None, None, :]
    )
    matches = matches & (
        first_side[:, :, None, None] + second_side[:, :, :, None] == first_side[:, None, None, :]
    )
    matches = matches & (partner_codes[:, :, :, None] % rows == own_codes[:, None, None, :] % rows)
    chosen = jnp.einsum(
        "qabs,qabxy->qasxy",
        matches.astype(jnp.bfloat16),
        partner,
        preferred_element_type=jnp.float32,
    ).astype(jnp.bfloat16)
    square = jnp.einsum("qaxy,qasyz->qsxz", tiles[0], chosen, preferred_element_type=jnp.float32)
    square_low = square.astype(jnp.bfloat16)
    cube = jnp.einsum("qaxy,qasyz->qsxz", square_low, chosen, preferred_element_type=jnp.float32)
    result = (3.0 * square_low.astype(jnp.float32) - 2.0 * cube).astype(jnp.bfloat16)
    return result.reshape((1, 1) + result.shape)


def neighbours(arrays):
    padded = (
        padded_2(arrays[0], (("row", 0), ("col", 1)), 1),
        padded_2(arrays[1], (("row", 0), ("col", 1)), 1),
        padded_2(arrays[2], (("row", 0), ("col", 1)), 1),
        padded_2(arrays[3], (("row", 0), ("col", 1)), 1),
        padded_2(arrays[4], (("row", 0), ("col", 1)), 1),
        padded_2(arrays[5], (("row", 0), ("col", 1)), 1),
    )
    return tuple(
        (jnp.stack([ext[1, 1], ext[0, 1], ext[2, 1], ext[1, 0], ext[1, 2]]) for ext in padded)
    )


def per_device(dens_a, dens_b, codes_a, codes_b, counts_a, counts_b):
    states = [dens_a, dens_b]
    for step in range(ITERS):
        fetched = neighbours((states[0], states[1], codes_a, codes_b, counts_a, counts_b))
        states = [
            purify_region(fetched[0], fetched[2], fetched[4]),
            purify_region(fetched[1], fetched[3], fetched[5]),
        ]
    return (states[0], states[1])


def solution(mesh):
    placed = (
        P("row", "col", None, None, None, None),
        P("row", "col", None, None, None, None),
        P("row", "col", None, None),
        P("row", "col", None, None),
        P("row", "col", None),
        P("row", "col", None),
    )
    return jax.shard_map(
        per_device,
        mesh=mesh,
        in_specs=placed,
        out_specs=(
            P("row", "col", None, None, None, None),
            P("row", "col", None, None, None, None),
        ),
        check_vma=False,
    )
```

profile of v0, /device:TPU:1, one launch (start us, length us, event | category | flops | bytes accessed | tf_op | source)
XLA Modules:
  0.0 363.5 jit_solution(7758545662032323601)
XLA Ops:
  0.7 5.5 %collective-permute-start.8 = (bf16[1,1,1,3,256,256]{5,4,3,2,1,0:T(8,128)(2,1)}, bf16[1,1,1,3,256,256]{5,4,3,2,1,0:T(8,128)(2,1)S(1)}, u32[]{:S(2)}, u32[]{:S(2)}) collective-permute-start(bf16[1,1,1,3,256,256]{5,4,3,2,1,0:T(8,128)(2,1)} %param.12), channel_id=1, source_target_pairs={{0,8},{8,16},{16,24},{24,32},{32,40},{40,48},{48,56},{56,64},{64,7... | collective-permute-start | bytes 1179656 | tf_op jit(solution)/shard_map/ppermute | solution.py:16
  6.2 5.3 %collective-permute-start.9 = (bf16[1,1,1,3,256,256]{5,4,3,2,1,0:T(8,128)(2,1)}, bf16[1,1,1,3,256,256]{5,4,3,2,1,0:T(8,128)(2,1)S(1)}, u32[]{:S(2)}, u32[]{:S(2)}) collective-permute-start(bf16[1,1,1,3,256,256]{5,4,3,2,1,0:T(8,128)(2,1)} %param.12), channel_id=1, source_target_pairs={{8,0},{16,8},{24,16},{32,24},{40,32},{48,40},{56,48},{64,56},{72,6... | collective-permute-start | bytes 1179656 | tf_op jit(solution)/shard_map/ppermute | solution.py:18
  11.5 1.9 collective-permute-start.4
  13.5 8.7 %collective-permute-start.5 = (s32[1,1,1,3]{3,2,1,0:T(1,128)}, s32[1,1,1,3]{3,2,1,0:T(1,128)S(1)}, u32[]{:S(2)}, u32[]{:S(2)}) collective-permute-start(s32[1,1,1,3]{3,2,1,0:T(1,128)} %param.14), channel_id=1, source_target_pairs={{8,0},{16,8},{24,16},{32,24},{40,32},{48,40},{56,48},{64,56},{72,6... | collective-permute-start | bytes 44 | tf_op jit(solution)/shard_map/ppermute | solution.py:18
  22.2 1.9 collective-permute-start
  30.6 1.8 bitcast_dynamic-update-slice_fusion.5
  33.1 7.9 %collective-permute-start.1 = (s32[1,1,1]{0,2,1:T(1,128)}, s32[1,1,1]{0,2,1:T(1,128)}, u32[]{:S(2)}, u32[]{:S(2)}) collective-permute-start(s32[1,1,1]{0,2,1:T(1,128)} %bitcast.3), channel_id=1, source_target_pairs={{8,0},{16,8},{24,16},{32,24},{40,32},{48,40},{56,48},{64,56},{72,6... | collective-permute-start | bytes 20 | tf_op jit(solution)/shard_map/ppermute | solution.py:18
  42.0 1.9 collective-permute-start.16
  45.2 5.9 %collective-permute-done.16 = s32[1,1,1]{0,2,1:T(1,128)} collective-permute-done((s32[1,1,1]{0,2,1:T(1,128)}, s32[1,1,1]{0,2,1:T(1,128)}, u32[]{:S(2)}, u32[]{:S(2)}) %collective-permute-start.16) | collective-permute-done | bytes 36 | tf_op jit(solution)/shard_map/ppermute | solution.py:16
  51.1 8.4 %collective-permute-start.17 = (s32[1,1,1]{0,2,1:T(1,128)}, s32[1,1,1]{0,2,1:T(1,128)}, u32[]{:S(2)}, u32[]{:S(2)}) collective-permute-start(s32[1,1,1]{0,2,1:T(1,128)} %bitcast.82), channel_id=1, source_target_pairs={{8,0},{16,8},{24,16},{32,24},{40,32},{48,40},{56,48},{64,56},{72,6... | collective-permute-start | bytes 20 | tf_op jit(solution)/shard_map/ppermute | solution.py:18
  60.4 1.9 collective-permute-start.24
  63.7 1.9 collective-permute-start.20
  67.1 12.6 %collective-permute-start.25 = (bf16[1,1,1,3,256,256]{5,4,3,2,1,0:T(8,128)(2,1)S(1)}, bf16[1,1,1,3,256,256]{5,4,3,2,1,0:T(8,128)(2,1)S(1)}, u32[]{:S(2)}, u32[]{:S(2)}) collective-permute-start(bf16[1,1,1,3,256,256]{5,4,3,2,1,0:T(8,128)(2,1)S(1)} %copy-done.1), channel_id=1, source_target_pairs={{8,0},{16,8},{24,16},{32,24},{40,32},{48,40},{56,48},{64,56},{72,6... | collective-permute-start | bytes 1179656 | tf_op jit(solution)/shard_map/ppermute | solution.py:18
  79.7 1.9 collective-permute-start.21
  81.7 2.9 collective-permute-done.21
  84.6 1.9 collective-permute-start.2
  86.5 4.4 %collective-permute-done.2 = s32[3,1,1]{0,2,1:T(1,128)S(1)} collective-permute-done((s32[3,1,1]{0,2,1:T(1,128)S(1)}, s32[3,1,1]{0,2,1:T(1,128)S(1)}, u32[]{:S(2)}, u32[]{:S(2)}) %collective-permute-start.2) | collective-permute-done | bytes 44 | tf_op jit(solution)/shard_map/ppermute | solution.py:16
  91.0 2.0 collective-permute-start.3
  95.3 1.9 collective-permute-start.18
  97.8 2.5 stack.28
  101.6 4.9 %collective-permute-start.19 = (s32[3,1,1]{0,2,1:T(1,128)S(1)}, s32[3,1,1]{0,2,1:T(1,128)S(1)}, u32[]{:S(2)}, u32[]{:S(2)}) collective-permute-start(s32[3,1,1]{0,2,1:T(1,128)S(1)} %pad_add_fusion.1), channel_id=1, source_target_pairs={{1,0},{2,1},{3,2},{4,3},{5,4},{6,5},{7,6},{0,7},{9,8},{10,9},{11,1... | collective-permute-start | bytes 44 | tf_op jit(solution)/shard_map/ppermute | solution.py:18
  107.2 2.1 collective-permute-start.6
  109.9 2.6 stack.32
  113.8 5.0 %collective-permute-start.7 = (s32[3,1,1,3]{3,2,1,0:T(1,128)S(1)}, s32[3,1,1,3]{3,2,1,0:T(1,128)S(1)}, u32[]{:S(2)}, u32[]{:S(2)}) collective-permute-start(s32[3,1,1,3]{3,2,1,0:T(1,128)S(1)} %constant_dynamic-update-slice_fusion), channel_id=1, source_target_pairs={{1,0},{2,1},{3,2},{4,3},{5,4},{6,5},{7,6},{0,7},{9,8},{10,9},{11,1... | collective-permute-start | bytes 116 | tf_op jit(solution)/shard_map/ppermute | solution.py:18
  119.5 1.9 collective-permute-start.22
  122.2 4.0 %collective-permute-done.22 = s32[3,1,1,3]{3,2,1,0:T(1,128)S(1)} collective-permute-done((s32[3,1,1,3]{3,2,1,0:T(1,128)S(1)}, s32[3,1,1,3]{3,2,1,0:T(1,128)S(1)}, u32[]{:S(2)}, u32[]{:S(2)}) %collective-permute-start.22) | collective-permute-done | bytes 68 | tf_op jit(solution)/shard_map/ppermute | solution.py:16
  126.2 3.4 collective-permute-start.23
  131.6 1.9 collective-permute-start.10
  133.5 5.5 %collective-permute-start.11 = (bf16[3,1,1,3,256,256]{5,4,3,2,1,0:T(8,128)(2,1)S(1)}, bf16[3,1,1,3,256,256]{5,4,3,2,1,0:T(8,128)(2,1)S(1)}, u32[]{:S(2)}, u32[]{:S(2)}) collective-permute-start(bf16[3,1,1,3,256,256]{5,4,3,2,1,0:T(8,128)(2,1)S(1)} %constant_dynamic-update-slice_fusion.8), channel_id=1, source_target_pairs={{1,0},{2,1},{3,2},{4,3},{5,4},{6,5},{7,6},{0,7},{9,8},{10,9},{11,1... | collective-permute-start | bytes 3538952 | tf_op jit(solution)/shard_map/ppermute | solution.py:18
  141.4 1.9 collective-permute-start.26
  143.3 5.5 %collective-permute-start.27 = (bf16[3,1,1,3,256,256]{5,4,3,2,1,0:T(8,128)(2,1)}, bf16[3,1,1,3,256,256]{5,4,3,2,1,0:T(8,128)(2,1)}, u32[]{:S(2)}, u32[]{:S(2)}) collective-permute-start(bf16[3,1,1,3,256,256]{5,4,3,2,1,0:T(8,128)(2,1)} %constant_dynamic-update-slice_fusion.19), channel_id=1, source_target_pairs={{1,0},{2,1},{3,2},{4,3},{5,4},{6,5},{7,6},{0,7},{9,8},{10,9},{11,1... | collective-permute-start | bytes 3538952 | tf_op jit(solution)/shard_map/ppermute | solution.py:18
  154.4 20.9 %collective-permute-done.11 = bf16[3,1,1,3,256,256]{5,4,3,2,1,0:T(8,128)(2,1)S(1)} collective-permute-done((bf16[3,1,1,3,256,256]{5,4,3,2,1,0:T(8,128)(2,1)S(1)}, bf16[3,1,1,3,256,256]{5,4,3,2,1,0:T(8,128)(2,1)S(1)}, u32[]{:S(2)}, u32[]{:S(2)}) %collective-permute-start.11) | collective-permute-done | bytes 1179680 | tf_op jit(solution)/shard_map/ppermute | solution.py:18
  176.1 2.2 gather_fusion.2
  181.6 19.4 %collective-permute-start.12 = (bf16[1,1,1,3,256,256]{4,5,3,2,1,0:T(8,128)(2,1)S(1)}, bf16[1,1,1,3,256,256]{4,5,3,2,1,0:T(8,128)(2,1)S(1)}, u32[]{:S(2)}, u32[]{:S(2)}) collective-permute-start(bf16[1,1,1,3,256,256]{4,5,3,2,1,0:T(8,128)(2,1)S(1)} %bitcast.438), channel_id=1, source_target_pairs={{0,8},{8,16},{16,24},{24,32},{32,40},{40,48},{48,56},{56,64},{64,7... | collective-permute-start | bytes 1179656 | tf_op jit(solution)/shard_map/ppermute | solution.py:16
  201.0 4.2 %collective-permute-start.13 = (bf16[1,1,1,3,256,256]{4,5,3,2,1,0:T(8,128)(2,1)S(1)}, bf16[1,1,1,3,256,256]{4,5,3,2,1,0:T(8,128)(2,1)S(1)}, u32[]{:S(2)}, u32[]{:S(2)}) collective-permute-start(bf16[1,1,1,3,256,256]{4,5,3,2,1,0:T(8,128)(2,1)S(1)} %bitcast.439), channel_id=1, source_target_pairs={{8,0},{16,8},{24,16},{32,24},{40,32},{48,40},{56,48},{64,56},{72,6... | collective-permute-start | bytes 1179656 | tf_op jit(solution)/shard_map/ppermute | solution.py:18
  207.0 23.3 %collective-permute-done.27 = bf16[3,1,1,3,256,256]{5,4,3,2,1,0:T(8,128)(2,1)} collective-permute-done((bf16[3,1,1,3,256,256]{5,4,3,2,1,0:T(8,128)(2,1)}, bf16[3,1,1,3,256,256]{5,4,3,2,1,0:T(8,128)(2,1)}, u32[]{:S(2)}, u32[]{:S(2)}) %collective-permute-start.27) | collective-permute-done | bytes 1179680 | tf_op jit(solution)/shard_map/ppermute | solution.py:18
  232.0 2.2 gather_fusion.6
  236.7 1.9 collective-permute-start.28
  238.6 12.0 %collective-permute-start.29 = (bf16[1,1,1,3,256,256]{4,5,3,2,1,0:T(8,128)(2,1)S(1)}, bf16[1,1,1,3,256,256]{4,5,3,2,1,0:T(8,128)(2,1)S(1)}, u32[]{:S(2)}, u32[]{:S(2)}) collective-permute-start(bf16[1,1,1,3,256,256]{4,5,3,2,1,0:T(8,128)(2,1)S(1)} %bitcast.436), channel_id=1, source_target_pairs={{8,0},{16,8},{24,16},{32,24},{40,32},{48,40},{56,48},{64,56},{72,6... | collective-permute-start | bytes 1179656 | tf_op jit(solution)/shard_map/ppermute | solution.py:18
  250.8 1.9 collective-permute-start.14
  252.7 5.5 %collective-permute-start.15 = (bf16[3,1,1,3,256,256]{4,5,3,2,1,0:T(8,128)(2,1)S(1)}, bf16[3,1,1,3,256,256]{4,5,3,2,1,0:T(8,128)(2,1)S(1)}, u32[]{:S(2)}, u32[]{:S(2)}) collective-permute-start(bf16[3,1,1,3,256,256]{4,5,3,2,1,0:T(8,128)(2,1)S(1)} %pad_maximum_fusion), channel_id=1, source_target_pairs={{1,0},{2,1},{3,2},{4,3},{5,4},{6,5},{7,6},{0,7},{9,8},{10,9},{11,1... | collective-permute-start | bytes 3538952 | tf_op jit(solution)/shard_map/ppermute | solution.py:18
  259.4 1.9 collective-permute-start.30
  261.3 5.7 %collective-permute-start.31 = (bf16[3,1,1,3,256,256]{4,5,3,2,1,0:T(8,128)(2,1)}, bf16[3,1,1,3,256,256]{4,5,3,2,1,0:T(8,128)(2,1)}, u32[]{:S(2)}, u32[]{:S(2)}) collective-permute-start(bf16[3,1,1,3,256,256]{4,5,3,2,1,0:T(8,128)(2,1)} %pad_maximum_fusion.1), channel_id=1, source_target_pairs={{1,0},{2,1},{3,2},{4,3},{5,4},{6,5},{7,6},{0,7},{9,8},{10,9},{11,1... | collective-permute-start | bytes 3538952 | tf_op jit(solution)/shard_map/ppermute | solution.py:18
  268.6 15.4 %collective-permute-done.14 = bf16[3,1,1,3,256,256]{4,5,3,2,1,0:T(8,128)(2,1)S(1)} collective-permute-done((bf16[3,1,1,3,256,256]{4,5,3,2,1,0:T(8,128)(2,1)S(1)}, bf16[3,1,1,3,256,256]{4,5,3,2,1,0:T(8,128)(2,1)S(1)}, u32[]{:S(2)}, u32[]{:S(2)}) %collective-permute-start.14) | collective-permute-done | bytes 1179680 | tf_op jit(solution)/shard_map/ppermute | solution.py:16
  284.8 22.0 %collective-permute-done.15 = bf16[3,1,1,3,256,256]{4,5,3,2,1,0:T(8,128)(2,1)S(1)} collective-permute-done((bf16[3,1,1,3,256,256]{4,5,3,2,1,0:T(8,128)(2,1)S(1)}, bf16[3,1,1,3,256,256]{4,5,3,2,1,0:T(8,128)(2,1)S(1)}, u32[]{:S(2)}, u32[]{:S(2)}) %collective-permute-start.15) | collective-permute-done | bytes 1179680 | tf_op jit(solution)/shard_map/ppermute | solution.py:18
  307.5 2.3 gather_fusion.3
  314.8 19.9 %collective-permute-done.30 = bf16[3,1,1,3,256,256]{4,5,3,2,1,0:T(8,128)(2,1)} collective-permute-done((bf16[3,1,1,3,256,256]{4,5,3,2,1,0:T(8,128)(2,1)}, bf16[3,1,1,3,256,256]{4,5,3,2,1,0:T(8,128)(2,1)}, u32[]{:S(2)}, u32[]{:S(2)}) %collective-permute-start.30) | collective-permute-done | bytes 1179680 | tf_op jit(solution)/shard_map/ppermute | solution.py:16
  335.7 21.7 %collective-permute-done.31 = bf16[3,1,1,3,256,256]{4,5,3,2,1,0:T(8,128)(2,1)} collective-permute-done((bf16[3,1,1,3,256,256]{4,5,3,2,1,0:T(8,128)(2,1)}, bf16[3,1,1,3,256,256]{4,5,3,2,1,0:T(8,128)(2,1)}, u32[]{:S(2)}, u32[]{:S(2)}) %collective-permute-start.31) | collective-permute-done | bytes 1179680 | tf_op jit(solution)/shard_map/ppermute | solution.py:18
  (160 shorter events, 56.6 us)
Async XLA Ops:
  0.6 65.0 %copy-start.22 = (s32[1,1,1,3]{3,2,1,0:T(1,128)S(1)}, s32[1,1,1,3]{3,2,1,0:T(1,128)}, u32[]{:S(2)}) copy-start(s32[1,1,1,3]{3,2,1,0:T(1,128)} %param.14) | copy-start | bytes 40
  0.6 63.0 %copy-start.23 = (s32[1,1,1,3]{3,2,1,0:T(1,128)S(1)}, s32[1,1,1,3]{3,2,1,0:T(1,128)}, u32[]{:S(2)}) copy-start(s32[1,1,1,3]{3,2,1,0:T(1,128)} %param.15) | copy-start | bytes 40
  0.7 59.8 %copy-start.1 = (bf16[1,1,1,3,256,256]{5,4,3,2,1,0:T(8,128)(2,1)S(1)}, bf16[1,1,1,3,256,256]{5,4,3,2,1,0:T(8,128)(2,1)}, u32[]{:S(2)}) copy-start(bf16[1,1,1,3,256,256]{5,4,3,2,1,0:T(8,128)(2,1)} %param.13) | copy-start | bytes 1179652
  0.7 130.8 %collective-permute-start.8 = (bf16[1,1,1,3,256,256]{5,4,3,2,1,0:T(8,128)(2,1)}, bf16[1,1,1,3,256,256]{5,4,3,2,1,0:T(8,128)(2,1)S(1)}, u32[]{:S(2)}, u32[]{:S(2)}) collective-permute-start(bf16[1,1,1,3,256,256]{5,4,3,2,1,0:T(8,128)(2,1)} %param.12), channel_id=1, source_target_pairs={{0,8},{8,16},{16,24},{24,32},{32,40},{40,48},{48,56},{56,64},{64,7... | collective-permute-start | bytes 1179656 | tf_op jit(solution)/shard_map/ppermute | solution.py:16
  6.2 125.3 %collective-permute-start.9 = (bf16[1,1,1,3,256,256]{5,4,3,2,1,0:T(8,128)(2,1)}, bf16[1,1,1,3,256,256]{5,4,3,2,1,0:T(8,128)(2,1)S(1)}, u32[]{:S(2)}, u32[]{:S(2)}) collective-permute-start(bf16[1,1,1,3,256,256]{5,4,3,2,1,0:T(8,128)(2,1)} %param.12), channel_id=1, source_target_pairs={{8,0},{16,8},{24,16},{32,24},{40,32},{48,40},{56,48},{64,56},{72,6... | collective-permute-start | bytes 1179656 | tf_op jit(solution)/shard_map/ppermute | solution.py:18
  11.5 52.1 %collective-permute-start.4 = (s32[1,1,1,3]{3,2,1,0:T(1,128)}, s32[1,1,1,3]{3,2,1,0:T(1,128)S(1)}, u32[]{:S(2)}, u32[]{:S(2)}) collective-permute-start(s32[1,1,1,3]{3,2,1,0:T(1,128)} %param.14), channel_id=1, source_target_pairs={{0,8},{8,16},{16,24},{24,32},{32,40},{40,48},{48,56},{56,64},{64,7... | collective-permute-start | bytes 44 | tf_op jit(solution)/shard_map/ppermute | solution.py:16
  13.5 66.3 %collective-permute-start.5 = (s32[1,1,1,3]{3,2,1,0:T(1,128)}, s32[1,1,1,3]{3,2,1,0:T(1,128)S(1)}, u32[]{:S(2)}, u32[]{:S(2)}) collective-permute-start(s32[1,1,1,3]{3,2,1,0:T(1,128)} %param.14), channel_id=1, source_target_pairs={{8,0},{16,8},{24,16},{32,24},{40,32},{48,40},{56,48},{64,56},{72,6... | collective-permute-start | bytes 44 | tf_op jit(solution)/shard_map/ppermute | solution.py:18
  22.2 10.9 %collective-permute-start = (s32[1,1,1]{0,2,1:T(1,128)}, s32[1,1,1]{0,2,1:T(1,128)}, u32[]{:S(2)}, u32[]{:S(2)}) collective-permute-start(s32[1,1,1]{0,2,1:T(1,128)} %bitcast.3), channel_id=1, source_target_pairs={{0,8},{8,16},{16,24},{24,32},{32,40},{40,48},{48,56},{56,64},{64,7... | collective-permute-start | bytes 20 | tf_op jit(solution)/shard_map/ppermute | solution.py:16
  25.9 105.6 %copy-start = (bf16[1,1,1,3,256,256]{5,4,3,2,1,0:T(8,128)(2,1)S(1)}, bf16[1,1,1,3,256,256]{5,4,3,2,1,0:T(8,128)(2,1)}, u32[]{:S(2)}) copy-start(bf16[1,1,1,3,256,256]{5,4,3,2,1,0:T(8,128)(2,1)} %param.12) | copy-start | bytes 1179652
  27.2 151.1 %copy-start.17 = (pred[3]{0:T(512)(128)(4,1)}, pred[3]{0:T(512)(128)(4,1)S(1)}, u32[]{:S(2)}) copy-start(pred[3]{0:T(512)(128)(4,1)S(1)} %fusion.66) | copy-start | bytes 13
  29.9 204.3 %copy-start.15 = (pred[3]{0:T(512)(128)(4,1)}, pred[3]{0:T(512)(128)(4,1)S(1)}, u32[]{:S(2)}) copy-start(pred[3]{0:T(512)(128)(4,1)S(1)} %fusion.67) | copy-start | bytes 13
  30.5 145.6 %copy-start.5 = (s32[1024]{0:T(1024)}, s32[1024]{0:T(1024)S(1)}, u32[]{:S(2)}) copy-start(s32[1024]{0:T(1024)S(1)} %pad_clamp_fusion.1) | copy-start | bytes 12292
  30.6 147.9 %copy-start.21 = (pred[3]{0:T(512)(128)(4,1)}, pred[3]{0:T(512)(128)(4,1)S(1)}, u32[]{:S(2)}) copy-start(pred[3]{0:T(512)(128)(4,1)S(1)} %iota_compare_fusion.3) | copy-start | bytes 13
  32.4 199.6 %copy-start.4 = (s32[1024]{0:T(1024)}, s32[1024]{0:T(1024)S(1)}, u32[]{:S(2)}) copy-start(s32[1024]{0:T(1024)S(1)} %pad_clamp_fusion) | copy-start | bytes 12292
  33.0 201.3 %copy-start.19 = (pred[3]{0:T(512)(128)(4,1)}, pred[3]{0:T(512)(128)(4,1)S(1)}, u32[]{:S(2)}) copy-start(pred[3]{0:T(512)(128)(4,1)S(1)} %iota_compare_fusion.2) | copy-start | bytes 13
  33.1 8.9 %collective-permute-start.1 = (s32[1,1,1]{0,2,1:T(1,128)}, s32[1,1,1]{0,2,1:T(1,128)}, u32[]{:S(2)}, u32[]{:S(2)}) collective-permute-start(s32[1,1,1]{0,2,1:T(1,128)} %bitcast.3), channel_id=1, source_target_pairs={{8,0},{16,8},{24,16},{32,24},{40,32},{48,40},{56,48},{64,56},{72,6... | collective-permute-start | bytes 20 | tf_op jit(solution)/shard_map/ppermute | solution.py:18
  42.0 9.1 %collective-permute-start.16 = (s32[1,1,1]{0,2,1:T(1,128)}, s32[1,1,1]{0,2,1:T(1,128)}, u32[]{:S(2)}, u32[]{:S(2)}) collective-permute-start(s32[1,1,1]{0,2,1:T(1,128)} %bitcast.82), channel_id=1, source_target_pairs={{0,8},{8,16},{16,24},{24,32},{32,40},{40,48},{48,56},{56,64},{64,7... | collective-permute-start | bytes 20 | tf_op jit(solution)/shard_map/ppermute | solution.py:16
  51.1 9.4 %collective-permute-start.17 = (s32[1,1,1]{0,2,1:T(1,128)}, s32[1,1,1]{0,2,1:T(1,128)}, u32[]{:S(2)}, u32[]{:S(2)}) collective-permute-start(s32[1,1,1]{0,2,1:T(1,128)} %bitcast.82), channel_id=1, source_target_pairs={{8,0},{16,8},{24,16},{32,24},{40,32},{48,40},{56,48},{64,56},{72,6... | collective-permute-start | bytes 20 | tf_op jit(solution)/shard_map/ppermute | solution.py:18
  60.4 78.5 %collective-permute-start.24 = (bf16[1,1,1,3,256,256]{5,4,3,2,1,0:T(8,128)(2,1)S(1)}, bf16[1,1,1,3,256,256]{5,4,3,2,1,0:T(8,128)(2,1)S(1)}, u32[]{:S(2)}, u32[]{:S(2)}) collective-permute-start(bf16[1,1,1,3,256,256]{5,4,3,2,1,0:T(8,128)(2,1)S(1)} %copy-done.1), channel_id=1, source_target_pairs={{0,8},{8,16},{16,24},{24,32},{32,40},{40,48},{48,56},{56,64},{64,7... | collective-permute-start | bytes 1179656 | tf_op jit(solution)/shard_map/ppermute | solution.py:16
  63.7 3.4 collective-permute-start.20
  65.6 112.9 %copy-start.13 = (s32[3]{0:T(128)}, s32[3]{0:T(128)S(1)}, u32[]{:S(2)}) copy-start(s32[3]{0:T(128)S(1)} %get-tuple-element.20) | copy-start | bytes 40
  65.6 112.9 %copy-start.14 = (s32[3]{0:T(128)}, s32[3]{0:T(128)S(1)}, u32[]{:S(2)}) copy-start(s32[3]{0:T(128)S(1)} %get-tuple-element.22) | copy-start | bytes 40
  67.1 73.4 %collective-permute-start.25 = (bf16[1,1,1,3,256,256]{5,4,3,2,1,0:T(8,128)(2,1)S(1)}, bf16[1,1,1,3,256,256]{5,4,3,2,1,0:T(8,128)(2,1)S(1)}, u32[]{:S(2)}, u32[]{:S(2)}) collective-permute-start(bf16[1,1,1,3,256,256]{5,4,3,2,1,0:T(8,128)(2,1)S(1)} %copy-done.1), channel_id=1, source_target_pairs={{8,0},{16,8},{24,16},{32,24},{40,32},{48,40},{56,48},{64,56},{72,6... | collective-permute-start | bytes 1179656 | tf_op jit(solution)/shard_map/ppermute | solution.py:18
  79.7 154.7 %copy-start.9 = (s32[3]{0:T(128)}, s32[3]{0:T(128)S(1)}, u32[]{:S(2)}) copy-start(s32[3]{0:T(128)S(1)} %get-tuple-element.17) | copy-start | bytes 40
  79.7 154.7 %copy-start.11 = (s32[3]{0:T(128)}, s32[3]{0:T(128)S(1)}, u32[]{:S(2)}) copy-start(s32[3]{0:T(128)S(1)} %get-tuple-element.19) | copy-start | bytes 40
  79.7 4.9 %collective-permute-start.21 = (s32[1,1,1,3]{3,2,1,0:T(1,128)S(1)}, s32[1,1,1,3]{3,2,1,0:T(1,128)S(1)}, u32[]{:S(2)}, u32[]{:S(2)}) collective-permute-start(s32[1,1,1,3]{3,2,1,0:T(1,128)S(1)} %copy-done.23), channel_id=1, source_target_pairs={{8,0},{16,8},{24,16},{32,24},{40,32},{48,40},{56,48},{64,56},{72,6... | collective-permute-start | bytes 44 | tf_op jit(solution)/shard_map/ppermute | solution.py:18
  84.6 6.4 %collective-permute-start.2 = (s32[3,1,1]{0,2,1:T(1,128)S(1)}, s32[3,1,1]{0,2,1:T(1,128)S(1)}, u32[]{:S(2)}, u32[]{:S(2)}) collective-permute-start(s32[3,1,1]{0,2,1:T(1,128)S(1)} %pad_add_fusion), channel_id=1, source_target_pairs={{0,1},{1,2},{2,3},{3,4},{4,5},{5,6},{6,7},{7,0},{8,9},{9,10},{10,1... | collective-permute-start | bytes 44 | tf_op jit(solution)/shard_map/ppermute | solution.py:16
  91.0 4.3 %collective-permute-start.3 = (s32[3,1,1]{0,2,1:T(1,128)S(1)}, s32[3,1,1]{0,2,1:T(1,128)S(1)}, u32[]{:S(2)}, u32[]{:S(2)}) collective-permute-start(s32[3,1,1]{0,2,1:T(1,128)S(1)} %pad_add_fusion), channel_id=1, source_target_pairs={{1,0},{2,1},{3,2},{4,3},{5,4},{6,5},{7,6},{0,7},{9,8},{10,9},{11,1... | collective-permute-start | bytes 44 | tf_op jit(solution)/shard_map/ppermute | solution.py:18
  95.3 6.4 %collective-permute-start.18 = (s32[3,1,1]{0,2,1:T(1,128)S(1)}, s32[3,1,1]{0,2,1:T(1,128)S(1)}, u32[]{:S(2)}, u32[]{:S(2)}) collective-permute-start(s32[3,1,1]{0,2,1:T(1,128)S(1)} %pad_add_fusion.1), channel_id=1, source_target_pairs={{0,1},{1,2},{2,3},{3,4},{4,5},{5,6},{6,7},{7,0},{8,9},{9,10},{10,1... | collective-permute-start | bytes 44 | tf_op jit(solution)/shard_map/ppermute | solution.py:16
  101.6 5.6 %collective-permute-start.19 = (s32[3,1,1]{0,2,1:T(1,128)S(1)}, s32[3,1,1]{0,2,1:T(1,128)S(1)}, u32[]{:S(2)}, u32[]{:S(2)}) collective-permute-start(s32[3,1,1]{0,2,1:T(1,128)S(1)} %pad_add_fusion.1), channel_id=1, source_target_pairs={{1,0},{2,1},{3,2},{4,3},{5,4},{6,5},{7,6},{0,7},{9,8},{10,9},{11,1... | collective-permute-start | bytes 44 | tf_op jit(solution)/shard_map/ppermute | solution.py:18
  107.2 6.6 %collective-permute-start.6 = (s32[3,1,1,3]{3,2,1,0:T(1,128)S(1)}, s32[3,1,1,3]{3,2,1,0:T(1,128)S(1)}, u32[]{:S(2)}, u32[]{:S(2)}) collective-permute-start(s32[3,1,1,3]{3,2,1,0:T(1,128)S(1)} %constant_dynamic-update-slice_fusion), channel_id=1, source_target_pairs={{0,1},{1,2},{2,3},{3,4},{4,5},{5,6},{6,7},{7,0},{8,9},{9,10},{10,1... | collective-permute-start | bytes 116 | tf_op jit(solution)/shard_map/ppermute | solution.py:16
  113.2 65.3 %copy-start.8 = (pred[3,3]{1,0:T(4,128)(4,1)}, pred[3,3]{1,0:T(4,128)(4,1)S(1)}, u32[]{:S(2)}) copy-start(pred[3,3]{1,0:T(4,128)(4,1)S(1)} %fusion.52) | copy-start | bytes 31
  113.3 121.1 %copy-start.6 = (pred[3,3]{1,0:T(4,128)(4,1)}, pred[3,3]{1,0:T(4,128)(4,1)S(1)}, u32[]{:S(2)}) copy-start(pred[3,3]{1,0:T(4,128)(4,1)S(1)} %fusion.53) | copy-start | bytes 31
  113.8 5.7 %collective-permute-start.7 = (s32[3,1,1,3]{3,2,1,0:T(1,128)S(1)}, s32[3,1,1,3]{3,2,1,0:T(1,128)S(1)}, u32[]{:S(2)}, u32[]{:S(2)}) collective-permute-start(s32[3,1,1,3]{3,2,1,0:T(1,128)S(1)} %constant_dynamic-update-slice_fusion), channel_id=1, source_target_pairs={{1,0},{2,1},{3,2},{4,3},{5,4},{6,5},{7,6},{0,7},{9,8},{10,9},{11,1... | collective-permute-start | bytes 116 | tf_op jit(solution)/shard_map/ppermute | solution.py:18
  119.5 6.7 %collective-permute-start.22 = (s32[3,1,1,3]{3,2,1,0:T(1,128)S(1)}, s32[3,1,1,3]{3,2,1,0:T(1,128)S(1)}, u32[]{:S(2)}, u32[]{:S(2)}) collective-permute-start(s32[3,1,1,3]{3,2,1,0:T(1,128)S(1)} %constant_dynamic-update-slice_fusion.11), channel_id=1, source_target_pairs={{0,1},{1,2},{2,3},{3,4},{4,5},{5,6},{6,7},{7,0},{8,9},{9,10},{10,1... | collective-permute-start | bytes 116 | tf_op jit(solution)/shard_map/ppermute | solution.py:16
  126.2 4.3 %collective-permute-start.23 = (s32[3,1,1,3]{3,2,1,0:T(1,128)S(1)}, s32[3,1,1,3]{3,2,1,0:T(1,128)S(1)}, u32[]{:S(2)}, u32[]{:S(2)}) collective-permute-start(s32[3,1,1,3]{3,2,1,0:T(1,128)S(1)} %constant_dynamic-update-slice_fusion.11), channel_id=1, source_target_pairs={{1,0},{2,1},{3,2},{4,3},{5,4},{6,5},{7,6},{0,7},{9,8},{10,9},{11,1... | collective-permute-start | bytes 116 | tf_op jit(solution)/shard_map/ppermute | solution.py:18
  131.6 22.1 %collective-permute-start.10 = (bf16[3,1,1,3,256,256]{5,4,3,2,1,0:T(8,128)(2,1)S(1)}, bf16[3,1,1,3,256,256]{5,4,3,2,1,0:T(8,128)(2,1)S(1)}, u32[]{:S(2)}, u32[]{:S(2)}) collective-permute-start(bf16[3,1,1,3,256,256]{5,4,3,2,1,0:T(8,128)(2,1)S(1)} %constant_dynamic-update-slice_fusion.8), channel_id=1, source_target_pairs={{0,1},{1,2},{2,3},{3,4},{4,5},{5,6},{6,7},{7,0},{8,9},{9,10},{10,1... | collective-permute-start | bytes 3538952 | tf_op jit(solution)/shard_map/ppermute | solution.py:16
  133.5 41.9 %collective-permute-start.11 = (bf16[3,1,1,3,256,256]{5,4,3,2,1,0:T(8,128)(2,1)S(1)}, bf16[3,1,1,3,256,256]{5,4,3,2,1,0:T(8,128)(2,1)S(1)}, u32[]{:S(2)}, u32[]{:S(2)}) collective-permute-start(bf16[3,1,1,3,256,256]{5,4,3,2,1,0:T(8,128)(2,1)S(1)} %constant_dynamic-update-slice_fusion.8), channel_id=1, source_target_pairs={{1,0},{2,1},{3,2},{4,3},{5,4},{6,5},{7,6},{0,7},{9,8},{10,9},{11,1... | collective-permute-start | bytes 3538952 | tf_op jit(solution)/shard_map/ppermute | solution.py:18
  141.4 63.8 %collective-permute-start.26 = (bf16[3,1,1,3,256,256]{5,4,3,2,1,0:T(8,128)(2,1)}, bf16[3,1,1,3,256,256]{5,4,3,2,1,0:T(8,128)(2,1)}, u32[]{:S(2)}, u32[]{:S(2)}) collective-permute-start(bf16[3,1,1,3,256,256]{5,4,3,2,1,0:T(8,128)(2,1)} %constant_dynamic-update-slice_fusion.19), channel_id=1, source_target_pairs={{0,1},{1,2},{2,3},{3,4},{4,5},{5,6},{6,7},{7,0},{8,9},{9,10},{10,1... | collective-permute-start | bytes 3538952 | tf_op jit(solution)/shard_map/ppermute | solution.py:16
  143.3 86.9 %collective-permute-start.27 = (bf16[3,1,1,3,256,256]{5,4,3,2,1,0:T(8,128)(2,1)}, bf16[3,1,1,3,256,256]{5,4,3,2,1,0:T(8,128)(2,1)}, u32[]{:S(2)}, u32[]{:S(2)}) collective-permute-start(bf16[3,1,1,3,256,256]{5,4,3,2,1,0:T(8,128)(2,1)} %constant_dynamic-update-slice_fusion.19), channel_id=1, source_target_pairs={{1,0},{2,1},{3,2},{4,3},{5,4},{6,5},{7,6},{0,7},{9,8},{10,9},{11,1... | collective-permute-start | bytes 3538952 | tf_op jit(solution)/shard_map/ppermute | solution.py:18
  181.6 69.1 %collective-permute-start.12 = (bf16[1,1,1,3,256,256]{4,5,3,2,1,0:T(8,128)(2,1)S(1)}, bf16[1,1,1,3,256,256]{4,5,3,2,1,0:T(8,128)(2,1)S(1)}, u32[]{:S(2)}, u32[]{:S(2)}) collective-permute-start(bf16[1,1,1,3,256,256]{4,5,3,2,1,0:T(8,128)(2,1)S(1)} %bitcast.438), channel_id=1, source_target_pairs={{0,8},{8,16},{16,24},{24,32},{32,40},{40,48},{48,56},{56,64},{64,7... | collective-permute-start | bytes 1179656 | tf_op jit(solution)/shard_map/ppermute | solution.py:16
  201.0 49.6 %collective-permute-start.13 = (bf16[1,1,1,3,256,256]{4,5,3,2,1,0:T(8,128)(2,1)S(1)}, bf16[1,1,1,3,256,256]{4,5,3,2,1,0:T(8,128)(2,1)S(1)}, u32[]{:S(2)}, u32[]{:S(2)}) collective-permute-start(bf16[1,1,1,3,256,256]{4,5,3,2,1,0:T(8,128)(2,1)S(1)} %bitcast.439), channel_id=1, source_target_pairs={{8,0},{16,8},{24,16},{32,24},{40,32},{48,40},{56,48},{64,56},{72,6... | collective-permute-start | bytes 1179656 | tf_op jit(solution)/shard_map/ppermute | solution.py:18
  236.7 21.5 %collective-permute-start.28 = (bf16[1,1,1,3,256,256]{4,5,3,2,1,0:T(8,128)(2,1)S(1)}, bf16[1,1,1,3,256,256]{4,5,3,2,1,0:T(8,128)(2,1)S(1)}, u32[]{:S(2)}, u32[]{:S(2)}) collective-permute-start(bf16[1,1,1,3,256,256]{4,5,3,2,1,0:T(8,128)(2,1)S(1)} %bitcast.435), channel_id=1, source_target_pairs={{0,8},{8,16},{16,24},{24,32},{32,40},{40,48},{48,56},{56,64},{64,7... | collective-permute-start | bytes 1179656 | tf_op jit(solution)/shard_map/ppermute | solution.py:16
  238.6 19.6 %collective-permute-start.29 = (bf16[1,1,1,3,256,256]{4,5,3,2,1,0:T(8,128)(2,1)S(1)}, bf16[1,1,1,3,256,256]{4,5,3,2,1,0:T(8,128)(2,1)S(1)}, u32[]{:S(2)}, u32[]{:S(2)}) collective-permute-start(bf16[1,1,1,3,256,256]{4,5,3,2,1,0:T(8,128)(2,1)S(1)} %bitcast.436), channel_id=1, source_target_pairs={{8,0},{16,8},{24,16},{32,24},{40,32},{48,40},{56,48},{64,56},{72,6... | collective-permute-start | bytes 1179656 | tf_op jit(solution)/shard_map/ppermute | solution.py:18
  250.8 33.2 %collective-permute-start.14 = (bf16[3,1,1,3,256,256]{4,5,3,2,1,0:T(8,128)(2,1)S(1)}, bf16[3,1,1,3,256,256]{4,5,3,2,1,0:T(8,128)(2,1)S(1)}, u32[]{:S(2)}, u32[]{:S(2)}) collective-permute-start(bf16[3,1,1,3,256,256]{4,5,3,2,1,0:T(8,128)(2,1)S(1)} %pad_maximum_fusion), channel_id=1, source_target_pairs={{0,1},{1,2},{2,3},{3,4},{4,5},{5,6},{6,7},{7,0},{8,9},{9,10},{10,1... | collective-permute-start | bytes 3538952 | tf_op jit(solution)/shard_map/ppermute | solution.py:16
  252.7 54.0 %collective-permute-start.15 = (bf16[3,1,1,3,256,256]{4,5,3,2,1,0:T(8,128)(2,1)S(1)}, bf16[3,1,1,3,256,256]{4,5,3,2,1,0:T(8,128)(2,1)S(1)}, u32[]{:S(2)}, u32[]{:S(2)}) collective-permute-start(bf16[3,1,1,3,256,256]{4,5,3,2,1,0:T(8,128)(2,1)S(1)} %pad_maximum_fusion), channel_id=1, source_target_pairs={{1,0},{2,1},{3,2},{4,3},{5,4},{6,5},{7,6},{0,7},{9,8},{10,9},{11,1... | collective-permute-start | bytes 3538952 | tf_op jit(solution)/shard_map/ppermute | solution.py:18
  259.4 75.3 %collective-permute-start.30 = (bf16[3,1,1,3,256,256]{4,5,3,2,1,0:T(8,128)(2,1)}, bf16[3,1,1,3,256,256]{4,5,3,2,1,0:T(8,128)(2,1)}, u32[]{:S(2)}, u32[]{:S(2)}) collective-permute-start(bf16[3,1,1,3,256,256]{4,5,3,2,1,0:T(8,128)(2,1)} %pad_maximum_fusion.1), channel_id=1, source_target_pairs={{0,1},{1,2},{2,3},{3,4},{4,5},{5,6},{6,7},{7,0},{8,9},{9,10},{10,1... | collective-permute-start | bytes 3538952 | tf_op jit(solution)/shard_map/ppermute | solution.py:16
  261.3 96.1 %collective-permute-start.31 = (bf16[3,1,1,3,256,256]{4,5,3,2,1,0:T(8,128)(2,1)}, bf16[3,1,1,3,256,256]{4,5,3,2,1,0:T(8,128)(2,1)}, u32[]{:S(2)}, u32[]{:S(2)}) collective-permute-start(bf16[3,1,1,3,256,256]{4,5,3,2,1,0:T(8,128)(2,1)} %pad_maximum_fusion.1), channel_id=1, source_target_pairs={{1,0},{2,1},{3,2},{4,3},{5,4},{6,5},{7,6},{0,7},{9,8},{10,9},{11,1... | collective-permute-start | bytes 3538952 | tf_op jit(solution)/shard_map/ppermute | solution.py:18
  (8 other events, 113.1 us)
where the time goes:
time: 370 us; the launch traced here: 364 us
  starting transfers between devices  150 us (41%)
  waiting for transfers between devices  150 us (41%)
  local copies, waits for them, and re-layouts  42.5 us (11%)
  matrix products  10.2 us (3%)
  other arithmetic  7.64 us (2%)
    ppermute x16, starting transfers between devices, padded_2(): lax.ppermute(head, axis, [((i + 1) % count, i) for i in range(count)])  98.2 us
    ppermute x16, waiting for transfers between devices, padded_2(): lax.ppermute(head, axis, [((i + 1) % count, i) for i in range(count)])  96.2 us
    ppermute x16, waiting for transfers between devices, padded_2(): lax.ppermute(tail, axis, [(i, (i + 1) % count) for i in range(count)])  54 us
    ppermute x16, starting transfers between devices, padded_2(): lax.ppermute(tail, axis, [(i, (i + 1) % count) for i in range(count)])  51.9 us
    unnamed x78, local copies, waits for them, and re-layouts  17.5 us
    another operation x10, local copies, waits for them, and re-layouts, neighbours(): jnp.stack([ext[1, 1], ext[0, 1], ext[2, 1], ext[1, 0], ext[1, 2]])  9.69 us
  transfers between devices with their start and end apart: 32, of which 20 were waited for; matrix products, arithmetic and copies ran while one was open for 15% of the time, Pallas kernels for 0%

commit v1 on v0

v1 whole, which is shorter than its diff:
```python
import jax
import jax.numpy as jnp
from jax import lax
from jax.experimental import pallas as pl
from jax.experimental.pallas import tpu as pltpu
from jax.sharding import PartitionSpec as P

OUT_X, DIAG, OUT_Z, IN_X, IN_Z, NONE = range(6)
BESIDE = (OUT_X, OUT_Z, IN_X, IN_Z)
MESH = pl.DeviceIdType.MESH
EDGE = 256
SLOTS = 3
HELD = 16


def beside(name):
    return NONE + 1 + 2 * name


def names_of(codes_ref, count_ref, row_bit, col_bit):
    names = []
    for slot in range(SLOTS):
        code = codes_ref[slot]
        vertical = jnp.where(code - 1 == row_bit, OUT_Z, IN_Z)
        lateral = jnp.where(code - 3 == col_bit, OUT_X, IN_X)
        name = jnp.where(code == 0, DIAG, jnp.where(code <= 2, vertical, lateral))
        names.append(jnp.where(slot < count_ref[0], name, NONE))
    return names


def in_order(names):
    a, b, c = (names[slot] * 4 + slot for slot in range(SLOTS))
    a, b = jnp.minimum(a, b), jnp.maximum(a, b)
    b, c = jnp.minimum(b, c), jnp.maximum(b, c)
    a, b = jnp.minimum(a, b), jnp.maximum(a, b)
    return [v // 4 for v in (a, b, c)], [v % 4 for v in (a, b, c)]


def diagonal_first(order):
    first, second, third = order
    has = (first == DIAG) | (second == DIAG)
    return [jnp.where(has, DIAG, first), jnp.where(second == DIAG, first, second), third], has


def place(names, wanted):
    at = jnp.int32(SLOTS)
    for index in reversed(range(SLOTS)):
        at = jnp.where(names[index] == wanted, index, at)
    return at


def matmul(x, y):
    return jnp.dot(x, y, preferred_element_type=jnp.float32)


def kernel(
    dens_a, dens_b, codes_a, codes_b, count_a, count_b, out_a, out_b,
    loaded, swap_out, swap_in, meta_out, meta_in, *rest,
):
    held = {(step, region): rest[2 * step + region] for step in (0, 1) for region in (0, 1)}
    fresh = {(step, region): rest[4 + 2 * step + region] for step in (0, 1) for region in (0, 1)}
    back, load_sem, swap_send, swap_recv, meta_sem, halo_send, halo_recv, back_send, back_recv = rest[8:]
    row, col = lax.axis_index("row"), lax.axis_index("col")
    core, side = lax.rem(row, 2), lax.rem(col, 2)
    sibling = row + 1 - 2 * core
    step_row, step_col = 2 * core - 1, 2 * side - 1

    def wrapped(r, c):
        return (lax.rem(r + 64, 64), lax.rem(c + 8, 8))

    partner = (sibling, col - step_col)
    target = {
        (0, OUT_X): wrapped(sibling, col + 2 * step_col),
        (1, OUT_X): wrapped(sibling, col - 2 * step_col),
        (0, OUT_Z): wrapped(row + step_row, col),
        (1, OUT_Z): wrapped(row - 3 * step_row, col),
    }
    for region in (0, 1):
        target[region, IN_X] = target[region, IN_Z] = (sibling, col)

    loads = [
        pltpu.make_async_copy(dens_a, loaded.at[0], load_sem.at[0]),
        pltpu.make_async_copy(dens_b, loaded.at[1], load_sem.at[1]),
    ]
    for load in loads:
        load.start()
    barrier = pltpu.get_barrier_semaphore()
    greeted = (partner, (sibling, col), target[0, OUT_X], target[1, OUT_X], target[0, OUT_Z], target[1, OUT_Z])
    for device in greeted:
        pl.semaphore_signal(barrier, 1, device_id=device, device_id_type=MESH)

    names_a = names_of(codes_a, count_a, core, side)
    names_b = names_of(codes_b, count_b, core, side)
    mine = [jnp.where(side == 0, a, b) for a, b in zip(names_a, names_b)]
    theirs = [jnp.where(side == 0, b, a) for a, b in zip(names_a, names_b)]
    order_mine, _ = in_order(mine)
    order_theirs, slot_theirs = in_order(theirs)
    for index in range(SLOTS):
        meta_out[index] = order_theirs[index]

    def block(step, region, name):
        return held[step, region].at[name]

    def halo(step, region, name, which):
        landing = region if name in (OUT_Z, IN_Z) else 1 - region
        return pltpu.make_async_remote_copy(
            src_ref=block(step, region, name if which else DIAG),
            dst_ref=block(step, landing, beside(name) + which),
            send_sem=halo_send.at[step, region, name, which],
            recv_sem=halo_recv.at[step, landing, name],
            device_id=target[region, name],
            device_id_type=MESH,
        )

    def swap(index):
        return pltpu.make_async_remote_copy(
            src_ref=swap_out.at[index],
            dst_ref=swap_in.at[index],
            send_sem=swap_send.at[index],
            recv_sem=swap_recv.at[index],
            device_id=partner,
            device_id_type=MESH,
        )

    def returned(index):
        return pltpu.make_async_remote_copy(
            src_ref=fresh[1, 1].at[index],
            dst_ref=back.at[index],
            send_sem=back_send.at[index],
            recv_sem=back_recv.at[index],
            device_id=partner,
            device_id_type=MESH,
        )

    meta = pltpu.make_async_remote_copy(
        src_ref=meta_out,
        dst_ref=meta_in,
        send_sem=meta_sem.at[0],
        recv_sem=meta_sem.at[1],
        device_id=partner,
        device_id_type=MESH,
    )

    nothing = jnp.zeros((EDGE, EDGE), jnp.bfloat16)
    for region in (0, 1):
        for step in (0, 1):
            held[step, region][NONE] = nothing
            fresh[step, region][SLOTS] = nothing
    back[SLOTS] = nothing

    for load in loads:
        load.wait()
    for index in range(SLOTS):
        chosen = loaded[1 - side, slot_theirs[index]]
        swap_out[index] = jnp.where(order_theirs[index] == NONE, nothing, chosen)
    for name in range(NONE):
        at = place(mine, name)
        chosen = loaded[side, jnp.minimum(at, SLOTS - 1)]
        held[0, 0][name] = jnp.where(at == SLOTS, nothing, chosen)

    pl.semaphore_wait(barrier, len(greeted))
    meta.start()
    swap(0).start()
    halo(0, 0, OUT_X, 0).start()
    halo(0, 0, OUT_Z, 0).start()
    swap(1).start()
    halo(0, 0, OUT_X, 1).start()
    halo(0, 0, OUT_Z, 1).start()
    swap(2).start()
    for name in (IN_X, IN_Z):
        for which in (0, 1):
            halo(0, 0, name, which).start()

    meta.wait_recv()
    order_other = [meta_in[index] for index in range(SLOTS)]
    first, second, third = order_other

    swap(0).wait_recv()
    held[0, 1][OUT_X] = jnp.where(first == OUT_X, swap_in[0], nothing)
    halo(0, 1, OUT_X, 1).start()
    swap(1).wait_recv()
    held[0, 1][DIAG] = jnp.where(
        first == DIAG, swap_in[0], jnp.where(second == DIAG, swap_in[1], nothing)
    )
    for name in BESIDE:
        halo(0, 1, name, 0).start()
    swap(2).wait_recv()
    for name in (OUT_Z, IN_X, IN_Z):
        at = place(order_other, name)
        chosen = swap_in[jnp.minimum(at, SLOTS - 1)]
        held[0, 1][name] = jnp.where(at == SLOTS, nothing, chosen)
        halo(0, 1, name, 1).start()

    layout = [diagonal_first(order_mine), diagonal_first(order_other)]

    def arrived(step, region):
        for name in BESIDE:
            pair = held[step, region].at[pl.ds(beside(name), 2)]
            pltpu.make_async_copy(pair, pair, halo_recv.at[step, region, name]).wait()

    def purify(step, region, done):
        names, has = layout[region]

        def at(index):
            return held[step, region][index]

        none = [name == NONE for name in names]
        diagonal = at(DIAG)
        left = [at(name) for name in names]
        own = at(jnp.where(has, DIAG, jnp.where(none[0], NONE, beside(names[0]))))
        across = [None] + [at(jnp.where(none[i], NONE, beside(names[i]))) for i in (1, 2)]
        towards = [None] + [
            at(jnp.where(none[i] | jnp.logical_not(has), NONE, beside(names[i]) + 1)) for i in (1, 2)
        ]
        square = [
            matmul(left[0], own) + matmul(left[1], towards[1]) + matmul(left[2], towards[2]),
            matmul(diagonal, left[1]) + matmul(left[1], across[1]),
            matmul(diagonal, left[2]) + matmul(left[2], across[2]),
        ]
        low = [s.astype(jnp.bfloat16) for s in square]
        centre = jnp.where(has, low[0], nothing)
        for index in range(SLOTS):
            if index == 0:
                cube = matmul(low[0], own) + matmul(low[1], towards[1]) + matmul(low[2], towards[2])
            else:
                cube = matmul(centre, left[index]) + matmul(low[index], across[index])
            fresh[step, region][index] = (3.0 * low[index].astype(jnp.float32) - 2.0 * cube).astype(jnp.bfloat16)
            done(index)

    for region in (1, 0):
        arrived(0, region)
        purify(0, region, lambda index: None)
        for name in (DIAG, OUT_X, OUT_Z, IN_X, IN_Z):
            held[1, region][name] = fresh[0, region][place(layout[region][0], name)]
        for name in BESIDE:
            for which in (0, 1):
                halo(1, region, name, which).start()

    arrived(1, 1)
    purify(1, 1, lambda index: returned(index).start())
    arrived(1, 0)
    purify(1, 0, lambda index: None)

    def write(out, names, order, source):
        for slot in range(SLOTS):
            out[slot] = source(place(diagonal_first(order)[0], names[slot]))

    def own_result(index):
        return fresh[1, 0][index]

    def their_result(index):
        return back[index]

    @pl.when(side == 0)
    def _():
        write(out_a, mine, order_mine, own_result)

    @pl.when(side == 1)
    def _():
        write(out_b, mine, order_mine, own_result)

    for index in range(SLOTS):
        returned(index).wait_recv()

    @pl.when(side == 0)
    def _():
        write(out_b, theirs, order_theirs, their_result)

    @pl.when(side == 1)
    def _():
        write(out_a, theirs, order_theirs, their_result)

    meta.wait_send()
    for index in range(SLOTS):
        swap(index).wait_send()
        returned(index).wait_send()
    for step in (0, 1):
        for region in (0, 1):
            for name in BESIDE:
                for which in (0, 1):
                    halo(step, region, name, which).wait_send()


def per_device(dens_a, dens_b, codes_a, codes_b, counts_a, counts_b):
    stored = (SLOTS, EDGE, EDGE)
    shape = dens_a.shape
    in_vmem = pl.BlockSpec(memory_space=pltpu.VMEM)
    in_smem = pl.BlockSpec(memory_space=pltpu.SMEM)
    anywhere = pl.BlockSpec(memory_space=pl.ANY)
    new_a, new_b = pl.pallas_call(
        kernel,
        out_shape=[jax.ShapeDtypeStruct(stored, jnp.bfloat16)] * 2,
        in_specs=[anywhere, anywhere, in_smem, in_smem, in_smem, in_smem],
        out_specs=[in_vmem, in_vmem],
        scratch_shapes=[
            pltpu.VMEM((2, *stored), jnp.bfloat16),
            pltpu.VMEM(stored, jnp.bfloat16),
            pltpu.VMEM(stored, jnp.bfloat16),
            pltpu.SMEM((SLOTS,), jnp.int32),
            pltpu.SMEM((SLOTS,), jnp.int32),
            *[pltpu.VMEM((HELD, EDGE, EDGE), jnp.bfloat16)] * 4,
            *[pltpu.VMEM((SLOTS + 1, EDGE, EDGE), jnp.bfloat16)] * 5,
            pltpu.SemaphoreType.DMA((2,)),
            pltpu.SemaphoreType.DMA((SLOTS,)),
            pltpu.SemaphoreType.DMA((SLOTS,)),
            pltpu.SemaphoreType.DMA((2,)),
            pltpu.SemaphoreType.DMA((2, 2, NONE, 2)),
            pltpu.SemaphoreType.DMA((2, 2, NONE)),
            pltpu.SemaphoreType.DMA((SLOTS,)),
            pltpu.SemaphoreType.DMA((SLOTS,)),
        ],
        compiler_params=pltpu.CompilerParams(
            collective_id=0, has_side_effects=True, vmem_limit_bytes=40 * 2**20
        ),
        name="purify",
    )(
        dens_a.reshape(stored),
        dens_b.reshape(stored),
        codes_a.reshape(SLOTS),
        codes_b.reshape(SLOTS),
        counts_a.reshape(1),
        counts_b.reshape(1),
    )
    return new_a.reshape(shape), new_b.reshape(shape)


def solution(mesh):
    placed = (
        P("row", "col", None, None, None, None),
        P("row", "col", None, None, None, None),
        P("row", "col", None, None),
        P("row", "col", None, None),
        P("row", "col", None),
        P("row", "col", None),
    )
    return jax.shard_map(
        per_device,
        mesh=mesh,
        in_specs=placed,
        out_specs=(
            P("row", "col", None, None, None, None),
            P("row", "col", None, None, None, None),
        ),
        check_vma=False,
    )
```

time: 370 us -> 65.2 us (0.18); the launches traced: 364 us -> 64.9 us
  starting transfers between devices: 150 us -> 0 us
  waiting for transfers between devices: 150 us -> 0 us
  Pallas kernels: 0 us -> 58.8 us
  local copies, waits for them, and re-layouts: 42.5 us -> 4.14 us
  matrix products: 10.2 us -> 0 us
  other arithmetic: 7.64 us -> 0 us
    ppermute x32 -> x0, waiting for transfers between devices: 150 us -> none  [the longest x16 96.2 us: padded_2(): lax.ppermute(head, axis, [((i + 1) % count, i) for i in range(count)])]
    ppermute x32 -> x0, starting transfers between devices: 150 us -> none  [the longest x16 98.2 us: padded_2(): lax.ppermute(head, axis, [((i + 1) % count, i) for i in range(count)])]
    pallas_call x0 -> x1, Pallas kernels: none -> 58.8 us  [per_device(): pl.pallas_call(kernel, out_shape=[jax.ShapeDtypeStruct(stored, jnp.bfloat...]
    unnamed x78 -> x10, local copies, waits for them, and re-layouts: 17.5 us -> 4.14 us
    another operation x12 -> x0, local copies, waits for them, and re-layouts: 11.7 us -> none  [the longest x10 9.69 us: neighbours(): jnp.stack([ext[1, 1], ext[0, 1], ext[2, 1], ext[1, 0], ext[1, 2]])]
    dot_general x12 -> x0, matrix products: 10.2 us -> none  [the longest x4 5.14 us: purify_region(): jnp.einsum('qabs,qabxy->qasxy', matches.astype(jnp.bfloat16), partner, pr...]
    gather x8 -> x0, local copies, waits for them, and re-layouts: 9.76 us -> none  [the longest x4 7.37 us: purify_region(): partner = jnp.take(flat_tiles, own_codes, axis=0)]
    concatenate x4 -> x0, other arithmetic: 3.89 us -> none  [padded_2(): jnp.concatenate([lax.ppermute(tail, axis, [(i, (i + 1) % count) for i in...]
  transfers between devices with their start and end apart: 32 -> 0, of which waited for: 20 -> 0; matrix products, arithmetic and copies ran while one was open for 15% -> 0% of each run, Pallas kernels for 0% -> 0%
where the time goes in v1:
time: 65.2 us; the launch traced here: 64.9 us
  Pallas kernels  58.8 us (90%)
  local copies, waits for them, and re-layouts  4.14 us (6%)
  between operations  1.95 us (3%)
    pallas_call x1, Pallas kernels, per_device(): pl.pallas_call(kernel, out_shape=[jax.ShapeDtypeStruct(stored, jnp.bfloat...  58.8 us
    unnamed x10, local copies, waits for them, and re-layouts  4.14 us

profile of v1, /device:TPU:1, one launch (start us, length us, event | category | flops | bytes accessed | tf_op | source)
XLA Modules:
  0.0 64.9 jit_solution(8323450628303728517)
XLA Ops:
  1.9 0.0 copy-start.2
  1.9 0.0 copy-start.3
  1.9 0.6 copy-done.2
  2.6 0.0 copy-done.3
  2.6 0.0 copy-start
  2.6 1.0 %copy-done = bf16[1,1,1,3,256,256]{5,4,3,2,1,0:T(8,128)(2,1)S(1)} copy-done((bf16[1,1,1,3,256,256]{5,4,3,2,1,0:T(8,128)(2,1)S(1)}, bf16[1,1,1,3,256,256]{5,4,3,2,1,0:T(8,128)(2,1)}, u32[]{:S(2)}) %copy-start) | copy-done | bytes 393240
  3.6 0.0 copy-start.1
  3.6 1.0 %copy-done.1 = bf16[1,1,1,3,256,256]{5,4,3,2,1,0:T(8,128)(2,1)S(1)} copy-done((bf16[1,1,1,3,256,256]{5,4,3,2,1,0:T(8,128)(2,1)S(1)}, bf16[1,1,1,3,256,256]{5,4,3,2,1,0:T(8,128)(2,1)}, u32[]{:S(2)}) %copy-start.1) | copy-done | bytes 393240
  4.6 58.8 %purify.1 = (bf16[3,256,256]{2,1,0:T(8,128)(2,1)S(1)}, bf16[3,256,256]{2,1,0:T(8,128)(2,1)S(1)}) custom-call(bf16[3,256,256]{2,1,0:T(8,128)(2,1)S(1)} %bitcast.10, bf16[3,256,256]{2,1,0:T(8,128)(2,1)S(1)} %bitcast.11, s32[3]{0:T(128)S(1)} %bitcast.14, s32[3]{0:T(128)S(1)} %bitcast.15, s32[1]{0:T(128)} %bitcast.8.count_a, s32[1]{0:T(128)} %bitcast.9.count_b), custom_call_target="tpu_custom_call" | custom-call | tf_op jit(solution)/shard_map/purify/pallas_call | solution.py:290
  63.4 0.7 %copy.12 = bf16[1,1,1,3,256,256]{5,4,3,2,1,0:T(8,128)(2,1)} copy(bf16[1,1,1,3,256,256]{5,4,3,2,1,0:T(8,128)(2,1)S(1)} %bitcast.13) | data formatting | bytes 786432
  64.2 0.7 %copy.13 = bf16[1,1,1,3,256,256]{5,4,3,2,1,0:T(8,128)(2,1)} copy(bf16[1,1,1,3,256,256]{5,4,3,2,1,0:T(8,128)(2,1)S(1)} %bitcast.12) | data formatting | bytes 786432
Async XLA Ops:
  1.9 0.7 %copy-start.2 = (s32[1,1,1,3]{3,2,1,0:T(1,128)S(1)}, s32[1,1,1,3]{3,2,1,0:T(1,128)}, u32[]{:S(2)}) copy-start(s32[1,1,1,3]{3,2,1,0:T(1,128)} %param.8) | copy-start | bytes 40
  1.9 0.7 %copy-start.3 = (s32[1,1,1,3]{3,2,1,0:T(1,128)S(1)}, s32[1,1,1,3]{3,2,1,0:T(1,128)}, u32[]{:S(2)}) copy-start(s32[1,1,1,3]{3,2,1,0:T(1,128)} %param.9) | copy-start | bytes 40
  2.6 1.0 %copy-start = (bf16[1,1,1,3,256,256]{5,4,3,2,1,0:T(8,128)(2,1)S(1)}, bf16[1,1,1,3,256,256]{5,4,3,2,1,0:T(8,128)(2,1)}, u32[]{:S(2)}) copy-start(bf16[1,1,1,3,256,256]{5,4,3,2,1,0:T(8,128)(2,1)} %param.6) | copy-start | bytes 1179652
  3.6 1.0 %copy-start.1 = (bf16[1,1,1,3,256,256]{5,4,3,2,1,0:T(8,128)(2,1)S(1)}, bf16[1,1,1,3,256,256]{5,4,3,2,1,0:T(8,128)(2,1)}, u32[]{:S(2)}) copy-start(bf16[1,1,1,3,256,256]{5,4,3,2,1,0:T(8,128)(2,1)} %param.7) | copy-start | bytes 1179652

commit v2 on v1

--- a/solution.py
+++ b/solution.py
@@ -11,6 +11,7 @@
 EDGE = 256
 SLOTS = 3
 HELD = 16
+RELAYED = 192
 
 
 def beside(name):
@@ -54,12 +55,15 @@
 
 
 def kernel(
-    dens_a, dens_b, codes_a, codes_b, count_a, count_b, out_a, out_b,
-    loaded, swap_out, swap_in, meta_out, meta_in, *rest,
+    dens_a, dens_b, *given_and_rest,
 ):
+    given, (out_a, out_b), given_and_rest = given_and_rest[:4], given_and_rest[4:6], given_and_rest[6:]
+    kept, given_and_rest = given_and_rest[:4], given_and_rest[4:]
+    loaded, swap_out, swap_in, meta_out, meta_in, relay, *rest = given_and_rest
     held = {(step, region): rest[2 * step + region] for step in (0, 1) for region in (0, 1)}
     fresh = {(step, region): rest[4 + 2 * step + region] for step in (0, 1) for region in (0, 1)}
-    back, load_sem, swap_send, swap_recv, meta_sem, halo_send, halo_recv, back_send, back_recv = rest[8:]
+    back, load_sem, swap_send, swap_recv, meta_sem, halo_send, halo_recv, back_send, back_recv = rest[8:17]
+    relay_send, relay_recv, onward_send = rest[17:]
     row, col = lax.axis_index("row"), lax.axis_index("col")
     core, side = lax.rem(row, 2), lax.rem(col, 2)
     sibling = row + 1 - 2 * core
@@ -78,17 +82,41 @@
     for region in (0, 1):
         target[region, IN_X] = target[region, IN_Z] = (sibling, col)
 
+    depth = lax.rem(row // 2, 8)
+    first_plane, last_plane = depth == 0, depth == 7
+    edge = [(first_plane & (core == region)) | (last_plane & (core != region)) for region in (0, 1)]
+    across = tuple(jnp.where(edge[0], a, b) for a, b in zip(target[0, OUT_Z], target[1, OUT_Z]))
+    onward = (lax.rem(row + 16, 64), col)
+    behind = (lax.rem(row + 48, 64), col)
+    relay_of = (row - 14 + 1 - 2 * core, col)
+    relay_for = (row + 14 + 1 - 2 * core, col)
+
     loads = [
-        pltpu.make_async_copy(dens_a, loaded.at[0], load_sem.at[0]),
-        pltpu.make_async_copy(dens_b, loaded.at[1], load_sem.at[1]),
+        pltpu.make_async_copy(source, home, load_sem.at[index])
+        for index, (source, home) in enumerate(
+            [*zip(given, kept), (dens_a, loaded.at[0]), (dens_b, loaded.at[1])]
+        )
     ]
     for load in loads:
         load.start()
+    codes_a, codes_b, count_a, count_b = kept
     barrier = pltpu.get_barrier_semaphore()
-    greeted = (partner, (sibling, col), target[0, OUT_X], target[1, OUT_X], target[0, OUT_Z], target[1, OUT_Z])
-    for device in greeted:
+
+    def greet(device):
         pl.semaphore_signal(barrier, 1, device_id=device, device_id_type=MESH)
 
+    for device in (partner, (sibling, col), target[0, OUT_X], target[1, OUT_X]):
+        greet(device)
+    for region in (0, 1):
+        pl.when(jnp.logical_not(edge[region]))(lambda: greet(target[region, OUT_Z]))
+
+    @pl.when(first_plane)
+    def _():
+        greet(behind)
+        greet(relay_for)
+
+    for load in loads[:4]:
+        load.wait()
     names_a = names_of(codes_a, count_a, core, side)
     names_b = names_of(codes_b, count_b, core, side)
     mine = [jnp.where(side == 0, a, b) for a, b in zip(names_a, names_b)]
@@ -112,6 +140,69 @@
             device_id_type=MESH,
         )
 
+    def tail(ref):
+        return ref.at[pl.ds(EDGE - RELAYED, RELAYED)]
+
+    def head(ref):
+        return ref.at[pl.ds(0, EDGE - RELAYED)]
+
+    def halo_head(step, region):
+        return pltpu.make_async_remote_copy(
+            src_ref=head(block(step, region, OUT_Z)),
+            dst_ref=head(block(step, region, beside(OUT_Z) + 1)),
+            send_sem=halo_send.at[step, region, OUT_Z, 1],
+            recv_sem=halo_recv.at[step, region, OUT_Z],
+            device_id=target[region, OUT_Z],
+            device_id_type=MESH,
+        )
+
+    def to_relay(step, region):
+        return pltpu.make_async_remote_copy(
+            src_ref=tail(block(step, region, OUT_Z)),
+            dst_ref=relay.at[step],
+            send_sem=relay_send.at[step],
+            recv_sem=relay_recv.at[step],
+            device_id=relay_of,
+            device_id_type=MESH,
+        )
+
+    def from_relay(step, region):
+        return pltpu.make_async_remote_copy(
+            src_ref=relay.at[step],
+            dst_ref=tail(block(step, region, beside(OUT_Z) + 1)),
+            send_sem=onward_send.at[step],
+            recv_sem=halo_recv.at[step, region, OUT_Z],
+            device_id=onward,
+            device_id_type=MESH,
+        )
+
+    def parts(step, region, name, which):
+        whole = halo(step, region, name, which)
+        if name != OUT_Z or not which:
+            return [(None, whole)]
+        cut = edge[region] & last_plane
+        return [
+            (jnp.logical_not(cut), whole),
+            (cut, to_relay(step, region)),
+            (cut, halo_head(step, region)),
+        ]
+
+    def send(step, region, name, which, when=None):
+        for condition, copy in parts(step, region, name, which):
+            both = condition if when is None else when if condition is None else condition & when
+            if both is None:
+                copy.start()
+            else:
+                pl.when(both)(copy.start)
+
+    def pass_on(step):
+        for region in (0, 1):
+
+            @pl.when(first_plane & (core == region))
+            def _():
+                to_relay(step, region).wait_recv()
+                from_relay(step, region).start()
+
     def swap(index):
         return pltpu.make_async_remote_copy(
             src_ref=swap_out.at[index],
@@ -148,7 +239,7 @@
             fresh[step, region][SLOTS] = nothing
     back[SLOTS] = nothing
 
-    for load in loads:
+    for load in loads[4:]:
         load.wait()
     for index in range(SLOTS):
         chosen = loaded[1 - side, slot_theirs[index]]
@@ -158,18 +249,20 @@
         chosen = loaded[side, jnp.minimum(at, SLOTS - 1)]
         held[0, 0][name] = jnp.where(at == SLOTS, nothing, chosen)
 
-    pl.semaphore_wait(barrier, len(greeted))
+    pl.semaphore_wait(barrier, jnp.where(last_plane, 7, 6))
+    pl.when(first_plane | last_plane)(lambda: greet(across))
+    early = [jnp.logical_not(edge[region] & first_plane) for region in (0, 1)]
     meta.start()
     swap(0).start()
-    halo(0, 0, OUT_X, 0).start()
-    halo(0, 0, OUT_Z, 0).start()
+    send(0, 0, OUT_X, 0)
     swap(1).start()
-    halo(0, 0, OUT_X, 1).start()
-    halo(0, 0, OUT_Z, 1).start()
+    send(0, 0, OUT_X, 1)
     swap(2).start()
+    for which in (0, 1):
+        send(0, 0, OUT_Z, which, early[0])
     for name in (IN_X, IN_Z):
         for which in (0, 1):
-            halo(0, 0, name, which).start()
+            send(0, 0, name, which)
 
     meta.wait_recv()
     order_other = [meta_in[index] for index in range(SLOTS)]
@@ -177,19 +270,28 @@
 
     swap(0).wait_recv()
     held[0, 1][OUT_X] = jnp.where(first == OUT_X, swap_in[0], nothing)
-    halo(0, 1, OUT_X, 1).start()
+    send(0, 1, OUT_X, 1)
     swap(1).wait_recv()
     held[0, 1][DIAG] = jnp.where(
         first == DIAG, swap_in[0], jnp.where(second == DIAG, swap_in[1], nothing)
     )
     for name in BESIDE:
-        halo(0, 1, name, 0).start()
+        send(0, 1, name, 0, early[1] if name == OUT_Z else None)
     swap(2).wait_recv()
     for name in (OUT_Z, IN_X, IN_Z):
         at = place(order_other, name)
         chosen = swap_in[jnp.minimum(at, SLOTS - 1)]
         held[0, 1][name] = jnp.where(at == SLOTS, nothing, chosen)
-        halo(0, 1, name, 1).start()
+        send(0, 1, name, 1, early[1] if name == OUT_Z else None)
+
+    @pl.when(first_plane)
+    def _():
+        pl.semaphore_wait(barrier, 1)
+
+    for region in (0, 1):
+        for which in (0, 1):
+            pl.when(jnp.logical_not(early[region]))(halo(0, region, OUT_Z, which).start)
+    pass_on(0)
 
     layout = [diagonal_first(order_mine), diagonal_first(order_other)]
 
@@ -234,8 +336,9 @@
             held[1, region][name] = fresh[0, region][place(layout[region][0], name)]
         for name in BESIDE:
             for which in (0, 1):
-                halo(1, region, name, which).start()
-
+                send(1, region, name, which)
+
+    pass_on(1)
     arrived(1, 1)
     purify(1, 1, lambda index: returned(index).start())
     arrived(1, 0)
@@ -278,29 +381,38 @@
         for region in (0, 1):
             for name in BESIDE:
                 for which in (0, 1):
-                    halo(step, region, name, which).wait_send()
+                    for condition, copy in parts(step, region, name, which):
+                        if condition is None:
+                            copy.wait_send()
+                        else:
+                            pl.when(condition)(copy.wait_send)
+            pl.when(first_plane & (core == region))(from_relay(step, region).wait_send)
 
 
 def per_device(dens_a, dens_b, codes_a, codes_b, counts_a, counts_b):
     stored = (SLOTS, EDGE, EDGE)
     shape = dens_a.shape
     in_vmem = pl.BlockSpec(memory_space=pltpu.VMEM)
-    in_smem = pl.BlockSpec(memory_space=pltpu.SMEM)
-    anywhere = pl.BlockSpec(memory_space=pl.ANY)
+    in_hbm = pl.BlockSpec(memory_space=pltpu.HBM)
     new_a, new_b = pl.pallas_call(
         kernel,
         out_shape=[jax.ShapeDtypeStruct(stored, jnp.bfloat16)] * 2,
-        in_specs=[anywhere, anywhere, in_smem, in_smem, in_smem, in_smem],
+        in_specs=[in_hbm] * 6,
         out_specs=[in_vmem, in_vmem],
         scratch_shapes=[
+            pltpu.SMEM((SLOTS,), jnp.int32),
+            pltpu.SMEM((SLOTS,), jnp.int32),
+            pltpu.SMEM((1,), jnp.int32),
+            pltpu.SMEM((1,), jnp.int32),
             pltpu.VMEM((2, *stored), jnp.bfloat16),
             pltpu.VMEM(stored, jnp.bfloat16),
             pltpu.VMEM(stored, jnp.bfloat16),
             pltpu.SMEM((SLOTS,), jnp.int32),
             pltpu.SMEM((SLOTS,), jnp.int32),
+            pltpu.VMEM((2, RELAYED, EDGE), jnp.bfloat16),
             *[pltpu.VMEM((HELD, EDGE, EDGE), jnp.bfloat16)] * 4,
             *[pltpu.VMEM((SLOTS + 1, EDGE, EDGE), jnp.bfloat16)] * 5,
-            pltpu.SemaphoreType.DMA((2,)),
+            pltpu.SemaphoreType.DMA((6,)),
             pltpu.SemaphoreType.DMA((SLOTS,)),
             pltpu.SemaphoreType.DMA((SLOTS,)),
             pltpu.SemaphoreType.DMA((2,)),
@@ -308,9 +420,12 @@
             pltpu.SemaphoreType.DMA((2, 2, NONE)),
             pltpu.SemaphoreType.DMA((SLOTS,)),
             pltpu.SemaphoreType.DMA((SLOTS,)),
+            pltpu.SemaphoreType.DMA((2,)),
+            pltpu.SemaphoreType.DMA((2,)),
+            pltpu.SemaphoreType.DMA((2,)),
         ],
         compiler_params=pltpu.CompilerParams(
-            collective_id=0, has_side_effects=True, vmem_limit_bytes=40 * 2**20
+            collective_id=0, has_side_effects=True, vmem_limit_bytes=62 * 2**20
         ),
         name="purify",
     )(

time: 65.2 us -> 60.7 us (0.931)
  Pallas kernels: 58.8 us -> 55.9 us
  local copies, waits for them, and re-layouts: 4.14 us -> 2.57 us
    pallas_call x1, Pallas kernels: 58.8 us -> 55.9 us  [per_device(): pl.pallas_call(kernel, out_shape=[jax.ShapeDtypeStruct(stored, jnp.bfloat...]
    unnamed x10 -> x4, local copies, waits for them, and re-layouts: 4.14 us -> 2.57 us
where the time goes in v2:
time: 60.7 us; the launch traced here: 60.4 us
  Pallas kernels  55.9 us (92%)
  local copies, waits for them, and re-layouts  2.57 us (4%)
  between operations  1.94 us (3%)
    pallas_call x1, Pallas kernels, per_device(): pl.pallas_call(kernel, out_shape=[jax.ShapeDtypeStruct(stored, jnp.bfloat...  55.9 us
    unnamed x4, local copies, waits for them, and re-layouts  2.57 us

profile of v2, /device:TPU:1, one launch (start us, length us, event | category | flops | bytes accessed | tf_op | source)
XLA Modules:
  0.0 60.4 jit_solution(14949169913106690124)
XLA Ops:
  1.9 55.9 %purify.1 = (bf16[3,256,256]{2,1,0:T(8,128)(2,1)}, bf16[3,256,256]{2,1,0:T(8,128)(2,1)}) custom-call(bf16[3,256,256]{2,1,0:T(8,128)(2,1)} %bitcast.10, bf16[3,256,256]{2,1,0:T(8,128)(2,1)} %bitcast.11, s32[3]{0:T(128)} %bitcast.14, s32[3]{0:T(128)} %bitcast.15, s32[1]{0:T(128)} %bitcast.8.given_and_rest_2_, s32[1]{0:T(128)} %bitcast.9.given_and_rest_3_), custom_call_target="tpu_custom_call" | custom-call | tf_op jit(solution)/shard_map/purify/pallas_call | solution.py:397
  57.8 0.0 copy-start
  57.8 1.8 %copy.12 = bf16[1,1,1,3,256,256]{5,4,3,2,1,0:T(8,128)(2,1)} copy(bf16[1,1,1,3,256,256]{5,4,3,2,1,0:T(8,128)(2,1)} %bitcast.13) | data formatting | bytes 786432
  59.7 0.0 copy-done
  59.7 0.7 %copy.13 = bf16[1,1,1,3,256,256]{5,4,3,2,1,0:T(8,128)(2,1)} copy(bf16[1,1,1,3,256,256]{5,4,3,2,1,0:T(8,128)(2,1)S(1)} %bitcast.12) | data formatting | bytes 786432
Async XLA Ops:
  57.8 1.8 %copy-start = (bf16[3,256,256]{2,1,0:T(8,128)(2,1)S(1)}, bf16[3,256,256]{2,1,0:T(8,128)(2,1)}, u32[]{:S(2)}) copy-start(bf16[3,256,256]{2,1,0:T(8,128)(2,1)} %get-tuple-element.5) | copy-start | bytes 1179652

commit v3 on v1

v3 whole, which is shorter than its diff:
```python
import functools

import jax
import jax.numpy as jnp
from jax import lax
from jax.experimental import pallas as pl
from jax.experimental.pallas import tpu as pltpu
from jax.sharding import PartitionSpec as P

OUT_X, DIAG, OUT_Z, IN_X, IN_Z, NONE = range(6)
BESIDE = (OUT_X, OUT_Z, IN_X, IN_Z)
MESH = pl.DeviceIdType.MESH
EDGE = 256
SLOTS = 3
HELD = 16
RELAYED = 192


def beside(name):
    return NONE + 1 + 2 * name


def names_of(codes_ref, count_ref, row_bit, col_bit):
    names = []
    for slot in range(SLOTS):
        code = codes_ref[slot]
        vertical = jnp.where(code - 1 == row_bit, OUT_Z, IN_Z)
        lateral = jnp.where(code - 3 == col_bit, OUT_X, IN_X)
        name = jnp.where(code == 0, DIAG, jnp.where(code <= 2, vertical, lateral))
        names.append(jnp.where(slot < count_ref[0], name, NONE))
    return names


def in_order(names):
    a, b, c = (names[slot] * 4 + slot for slot in range(SLOTS))
    a, b = jnp.minimum(a, b), jnp.maximum(a, b)
    b, c = jnp.minimum(b, c), jnp.maximum(b, c)
    a, b = jnp.minimum(a, b), jnp.maximum(a, b)
    return [v // 4 for v in (a, b, c)], [v % 4 for v in (a, b, c)]


def diagonal_first(order):
    first, second, third = order
    has = (first == DIAG) | (second == DIAG)
    return [jnp.where(has, DIAG, first), jnp.where(second == DIAG, first, second), third], has


def place(names, wanted):
    at = jnp.int32(SLOTS)
    for index in reversed(range(SLOTS)):
        at = jnp.where(names[index] == wanted, index, at)
    return at


def matmul(x, y):
    return jnp.dot(x, y, preferred_element_type=jnp.float32)


def kernel(
    dens_a, dens_b, codes_a_hbm, codes_b_hbm, count_a_hbm, count_b_hbm, out_a, out_b,
    codes_a, codes_b, count_a, count_b, loaded, swap_out, swap_in, meta_out, meta_in, up, up_late, down, down_late,
    held_00, held_01, held_10, held_11, fresh_00, fresh_01, fresh_10, fresh_11, back,
    load_sem, swap_send, swap_recv, meta_sem, halo_send, halo_recv, back_send, back_recv, via_send, via_recv,
):
    held = ((held_00, held_01), (held_10, held_11))
    fresh = ((fresh_00, fresh_01), (fresh_10, fresh_11))
    row, col = lax.axis_index("row"), lax.axis_index("col")
    core, side = lax.rem(row, 2), lax.rem(col, 2)
    own = [core == region for region in (0, 1)]
    depth = lax.rem(row // 2, 8)
    first_plane, last_plane = depth == 0, depth == 7
    sibling = row + 1 - 2 * core
    step_col = 2 * side - 1

    def wrapped(r, c):
        return (lax.rem(r + 64, 64), lax.rem(c + 8, 8))

    partner = (sibling, col - step_col)
    target = {}
    for region in (0, 1):
        target[region, OUT_X] = wrapped(sibling, col + jnp.where(own[region], 2, -2) * step_col)
        target[region, OUT_Z] = wrapped(sibling + 4 * region - 2, col)
        target[region, IN_X] = target[region, IN_Z] = (sibling, col)
    across = tuple(jnp.where(first_plane, a, b) for a, b in zip(target[0, OUT_Z], target[1, OUT_Z]))
    onward, behind = wrapped(row + 16, col), wrapped(row - 16, col)
    relay_of, relay_for = wrapped(sibling - 14, col), wrapped(sibling + 14, col)

    loads = [
        pltpu.make_async_copy(source, home, load_sem.at[index])
        for index, (source, home) in enumerate(
            (
                (codes_a_hbm, codes_a),
                (codes_b_hbm, codes_b),
                (count_a_hbm, count_a),
                (count_b_hbm, count_b),
                (dens_a, loaded.at[0]),
                (dens_b, loaded.at[1]),
            )
        )
    ]
    for load in loads:
        load.start()
    barrier = pltpu.get_barrier_semaphore()

    def greet(device):
        pl.semaphore_signal(barrier, 1, device_id=device, device_id_type=MESH)

    for device in (partner, (sibling, col), target[0, OUT_X], target[1, OUT_X]):
        greet(device)
    pl.when(jnp.logical_not(first_plane))(lambda: greet(target[0, OUT_Z]))
    pl.when(jnp.logical_not(last_plane))(lambda: greet(target[1, OUT_Z]))

    pl.when(first_plane | last_plane)(lambda: greet(onward))
    pl.when(first_plane)(lambda: greet(behind))

    nothing = jnp.zeros((EDGE, EDGE), jnp.bfloat16)
    for region in (0, 1):
        for step in (0, 1):
            held[step][region][NONE] = nothing
            fresh[step][region][SLOTS] = nothing
    back[SLOTS] = nothing

    for load in loads[:4]:
        load.wait()
    names_a = names_of(codes_a, count_a, core, side)
    names_b = names_of(codes_b, count_b, core, side)
    mine = [jnp.where(side == 0, a, b) for a, b in zip(names_a, names_b)]
    theirs = [jnp.where(side == 0, b, a) for a, b in zip(names_a, names_b)]
    order_mine, _ = in_order(mine)
    order_theirs, slot_theirs = in_order(theirs)
    for index in range(SLOTS):
        meta_out[index] = order_theirs[index]

    def remote(source, landing, sent, received, device):
        return pltpu.make_async_remote_copy(
            src_ref=source,
            dst_ref=landing,
            send_sem=sent,
            recv_sem=received,
            device_id=device,
            device_id_type=MESH,
        )

    def swap(index):
        return remote(swap_out.at[index], swap_in.at[index], swap_send.at[index], swap_recv.at[index], partner)

    def returned(region, index):
        return remote(
            fresh[1][region].at[index], back.at[index], back_send.at[index], back_recv.at[index], partner
        )

    meta = remote(meta_out, meta_in, meta_sem.at[0], meta_sem.at[1], partner)

    def landing_of(region, name):
        return 1 - region if name in (OUT_Z, IN_Z) else region

    def halo(step, region, name, which, rows=slice(0, EDGE)):
        landing = landing_of(region, name)
        cut = pl.ds(rows.start, rows.stop - rows.start)
        return remote(
            held[step][region].at[name if which else DIAG, cut],
            held[step][landing].at[beside(name) + which, cut],
            halo_send.at[step, region, name, which],
            halo_recv.at[step, landing, name],
            target[region, name],
        )

    def up_first(which):
        source = held[0][1].at[OUT_Z if which else DIAG]
        return remote(source, up.at[which], halo_send.at[0, 1, OUT_Z, which], via_recv.at[which], relay_of)

    def up_first_on(which):
        landing = held[0][0].at[beside(OUT_Z) + which]
        return remote(up.at[which], landing, via_send.at[which], halo_recv.at[0, 0, OUT_Z], onward)

    tail = pl.ds(EDGE - RELAYED, RELAYED)

    def up_second():
        return remote(held[1][1].at[OUT_Z, tail], up_late, via_send.at[5], via_recv.at[2], relay_of)

    def up_second_on():
        landing = held[1][0].at[beside(OUT_Z) + 1, tail]
        return remote(up_late, landing, via_send.at[2], halo_recv.at[1, 0, OUT_Z], onward)

    def down_first(which):
        source = held[0][0].at[OUT_Z if which else DIAG]
        return remote(source, down.at[which], halo_send.at[0, 0, OUT_Z, which], via_recv.at[3 + which], behind)

    def down_first_on(which):
        landing = held[0][1].at[beside(OUT_Z) + which]
        return remote(down.at[which], landing, via_send.at[3 + which], halo_recv.at[0, 1, OUT_Z], relay_for)

    def down_second():
        return remote(held[1][0].at[OUT_Z], down_late, halo_send.at[1, 0, OUT_Z, 1], via_recv.at[5], relay_for)

    def down_second_on():
        landing = held[1][1].at[beside(OUT_Z) + 1]
        return remote(down_late, landing, via_send.at[6], halo_recv.at[1, 1, OUT_Z], behind)

    def parts(step, region, name, which):
        whole = halo(step, region, name, which)
        if name != OUT_Z:
            return [(None, whole)]
        if step == 0:
            other = [down_first, up_first][region](which)
            cut = first_plane if region == 0 else last_plane & own[1]
            return [(cut, other), (jnp.logical_not(cut), whole)]
        if which == 0:
            return [(None, whole)]
        if region == 0:
            return [(first_plane, down_second()), (jnp.logical_not(first_plane), whole)]
        return [
            (last_plane, up_second()),
            (last_plane, halo(step, region, name, which, slice(0, EDGE - RELAYED))),
            (jnp.logical_not(last_plane), whole),
        ]

    def send(step, region, name, which):
        for condition, copy in parts(step, region, name, which):
            if condition is None:
                copy.start()
            else:
                pl.when(condition)(copy.start)

    for load in loads[4:]:
        load.wait()
    for index in range(SLOTS):
        chosen = loaded[1 - side, slot_theirs[index]]
        swap_out[index] = jnp.where(order_theirs[index] == NONE, nothing, chosen)
    for region in (0, 1):

        @pl.when(own[region])
        def _():
            for name in range(NONE):
                at = place(mine, name)
                chosen = loaded[side, jnp.minimum(at, SLOTS - 1)]
                held[0][region][name] = jnp.where(at == SLOTS, nothing, chosen)

    pl.semaphore_wait(barrier, jnp.where(first_plane, 7, jnp.where(last_plane, 8, 6)))
    pl.when(first_plane | last_plane)(lambda: greet(across))
    pl.when(first_plane)(lambda: greet(relay_for))
    pl.when(last_plane)(lambda: greet(relay_of))
    meta.start()
    for region in (0, 1):

        @pl.when(own[region])
        def _():
            swap(0).start()
            send(0, region, OUT_X, 0)
            send(0, region, OUT_Z, 0)
            swap(1).start()
            send(0, region, OUT_X, 1)
            send(0, region, OUT_Z, 1)
            swap(2).start()
            for name in (IN_X, IN_Z):
                for which in (0, 1):
                    send(0, region, name, which)

    meta.wait_recv()
    order_other = [meta_in[index] for index in range(SLOTS)]
    first, second, third = order_other
    for region in (0, 1):

        @pl.when(jnp.logical_not(own[region]))
        def _():
            swap(0).wait_recv()
            held[0][region][OUT_X] = jnp.where(first == OUT_X, swap_in[0], nothing)
            send(0, region, OUT_X, 1)
            swap(1).wait_recv()
            held[0][region][DIAG] = jnp.where(
                first == DIAG, swap_in[0], jnp.where(second == DIAG, swap_in[1], nothing)
            )
            for name in (OUT_X, OUT_Z, IN_X, IN_Z):
                send(0, region, name, 0)
            swap(2).wait_recv()
            for name in (OUT_Z, IN_Z, IN_X):
                at = place(order_other, name)
                chosen = swap_in[jnp.minimum(at, SLOTS - 1)]
                held[0][region][name] = jnp.where(at == SLOTS, nothing, chosen)
                send(0, region, name, 1)

    @pl.when(first_plane)
    def _():
        pl.semaphore_wait(barrier, 2)
        for which in (0, 1):
            down_first(which).wait_recv()
            down_first_on(which).start()

    mine_first, mine_has = diagonal_first(order_mine)
    other_first, other_has = diagonal_first(order_other)
    layout = [
        (
            [jnp.where(own[region], a, b) for a, b in zip(mine_first, other_first)],
            (own[region] & mine_has) | (jnp.logical_not(own[region]) & other_has),
        )
        for region in (0, 1)
    ]

    def arrived(step, region):
        for name in BESIDE:
            pair = held[step][region].at[pl.ds(beside(name), 2)]
            pltpu.make_async_copy(pair, pair, halo_recv.at[step, region, name]).wait()

    def purify(step, region, done):
        names, has = layout[region]

        def at(index):
            return held[step][region][index]

        none = [name == NONE for name in names]
        diagonal = at(DIAG)
        left = [at(name) for name in names]
        right = at(jnp.where(has, DIAG, jnp.where(none[0], NONE, beside(names[0]))))
        over = [None] + [at(jnp.where(none[i], NONE, beside(names[i]))) for i in (1, 2)]
        towards = [None] + [
            at(jnp.where(none[i] | jnp.logical_not(has), NONE, beside(names[i]) + 1)) for i in (1, 2)
        ]
        square = [
            matmul(left[0], right) + matmul(left[1], towards[1]) + matmul(left[2], towards[2]),
            matmul(diagonal, left[1]) + matmul(left[1], over[1]),
            matmul(diagonal, left[2]) + matmul(left[2], over[2]),
        ]
        low = [s.astype(jnp.bfloat16) for s in square]
        centre = jnp.where(has, low[0], nothing)
        for index in range(SLOTS):
            if index == 0:
                cube = matmul(low[0], right) + matmul(low[1], towards[1]) + matmul(low[2], towards[2])
            else:
                cube = matmul(centre, left[index]) + matmul(low[index], over[index])
            fresh[step][region][index] = (3.0 * low[index].astype(jnp.float32) - 2.0 * cube).astype(jnp.bfloat16)
            done(index)

    def spread(region):
        for name in range(NONE):
            held[1][region][name] = fresh[0][region][place(layout[region][0], name)]
        for which in (0, 1):
            for name in (OUT_Z, OUT_X) if region else (OUT_X, OUT_Z):
                send(1, region, name, which)
        for name in (IN_X, IN_Z):
            for which in (0, 1):
                send(1, region, name, which)

    def give_back(region, index):
        pl.when(jnp.logical_not(own[region]))(returned(region, index).start)

    @pl.when(first_plane & own[0])
    def _():
        for which in (0, 1):
            up_first(which).wait_recv()
            up_first_on(which).start()

    arrived(0, 1)
    purify(0, 1, lambda index: None)
    spread(1)

    arrived(0, 0)
    purify(0, 0, lambda index: None)
    spread(0)

    @pl.when(first_plane)
    def _():
        up_second().wait_recv()
        up_second_on().start()

    @pl.when(last_plane)
    def _():
        down_second().wait_recv()
        down_second_on().start()

    for region in (1, 0):
        arrived(1, region)
        purify(1, region, functools.partial(give_back, region))

    def write(out, names, order, source):
        for slot in range(SLOTS):
            out[slot] = source[place(diagonal_first(order)[0], names[slot])]

    outs = (out_a, out_b)
    for which_side in (0, 1):
        for region in (0, 1):

            @pl.when((side == which_side) & own[region])
            def _():
                write(outs[which_side], mine, order_mine, fresh[1][region])

    for index in range(SLOTS):
        returned(0, index).wait_recv()
    for which_side in (0, 1):

        @pl.when(side == which_side)
        def _():
            write(outs[1 - which_side], theirs, order_theirs, back)

    meta.wait_send()
    for index in range(SLOTS):
        swap(index).wait_send()
        returned(0, index).wait_send()
    for step in (0, 1):
        for region in (0, 1):
            for name in BESIDE:
                for which in (0, 1):
                    for condition, copy in parts(step, region, name, which):
                        if condition is None:
                            copy.wait_send()
                        else:
                            pl.when(condition)(copy.wait_send)

    pl.when(last_plane)(down_second_on().wait_send)

    @pl.when(first_plane)
    def _():
        up_second_on().wait_send()
        for which in (0, 1):
            down_first_on(which).wait_send()
            pl.when(own[0])(up_first_on(which).wait_send)


def per_device(dens_a, dens_b, codes_a, codes_b, counts_a, counts_b):
    stored = (SLOTS, EDGE, EDGE)
    shape = dens_a.shape
    in_vmem = pl.BlockSpec(memory_space=pltpu.VMEM)
    in_hbm = pl.BlockSpec(memory_space=pltpu.HBM)
    new_a, new_b = pl.pallas_call(
        kernel,
        out_shape=[pltpu.VMEM(stored, jnp.bfloat16)] * 2,
        in_specs=[in_hbm] * 6,
        out_specs=[in_vmem, in_vmem],
        scratch_shapes=[
            pltpu.SMEM((SLOTS,), jnp.int32),
            pltpu.SMEM((SLOTS,), jnp.int32),
            pltpu.SMEM((1,), jnp.int32),
            pltpu.SMEM((1,), jnp.int32),
            pltpu.VMEM((2, *stored), jnp.bfloat16),
            pltpu.VMEM(stored, jnp.bfloat16),
            pltpu.VMEM(stored, jnp.bfloat16),
            pltpu.SMEM((SLOTS,), jnp.int32),
            pltpu.SMEM((SLOTS,), jnp.int32),
            pltpu.VMEM((2, EDGE, EDGE), jnp.bfloat16),
            pltpu.VMEM((RELAYED, EDGE), jnp.bfloat16),
            pltpu.VMEM((2, EDGE, EDGE), jnp.bfloat16),
            pltpu.VMEM((EDGE, EDGE), jnp.bfloat16),
            *[pltpu.VMEM((HELD, EDGE, EDGE), jnp.bfloat16)] * 4,
            *[pltpu.VMEM((SLOTS + 1, EDGE, EDGE), jnp.bfloat16)] * 5,
            pltpu.SemaphoreType.DMA((6,)),
            pltpu.SemaphoreType.DMA((SLOTS,)),
            pltpu.SemaphoreType.DMA((SLOTS,)),
            pltpu.SemaphoreType.DMA((2,)),
            pltpu.SemaphoreType.DMA((2, 2, NONE, 2)),
            pltpu.SemaphoreType.DMA((2, 2, NONE)),
            pltpu.SemaphoreType.DMA((SLOTS,)),
            pltpu.SemaphoreType.DMA((SLOTS,)),
            pltpu.SemaphoreType.DMA((7,)),
            pltpu.SemaphoreType.DMA((6,)),
        ],
        compiler_params=pltpu.CompilerParams(
            collective_id=0, has_side_effects=True, vmem_limit_bytes=60 * 2**20
        ),
        name="purify",
    )(
        dens_a.reshape(stored),
        dens_b.reshape(stored),
        codes_a.reshape(SLOTS),
        codes_b.reshape(SLOTS),
        counts_a.reshape(1),
        counts_b.reshape(1),
    )
    return new_a.reshape(shape), new_b.reshape(shape)


def solution(mesh):
    placed = (
        P("row", "col", None, None, None, None),
        P("row", "col", None, None, None, None),
        P("row", "col", None, None),
        P("row", "col", None, None),
        P("row", "col", None),
        P("row", "col", None),
    )
    return jax.shard_map(
        per_device,
        mesh=mesh,
        in_specs=placed,
        out_specs=(
            P("row", "col", None, None, None, None),
            P("row", "col", None, None, None, None),
        ),
        check_vma=False,
    )
```

time: 65.2 us -> 56.6 us (0.87)
  Pallas kernels: 58.8 us -> 52.4 us
  local copies, waits for them, and re-layouts: 4.14 us -> 1.49 us
    pallas_call x1, Pallas kernels: 58.8 us -> 52.4 us  [per_device(): pl.pallas_call(kernel, out_shape=[pltpu.VMEM(stored, jnp.bfloat16)] * 2,...]
    unnamed x10 -> x2, local copies, waits for them, and re-layouts: 4.14 us -> 1.49 us
where the time goes in v3:
time: 56.6 us; the launch traced here: 55.8 us
  Pallas kernels  52.4 us (93%)
  between operations  1.93 us (3%)
  local copies, waits for them, and re-layouts  1.49 us (3%)
    pallas_call x1, Pallas kernels, per_device(): pl.pallas_call(kernel, out_shape=[pltpu.VMEM(stored, jnp.bfloat16)] * 2,...  52.4 us
    unnamed x2, local copies, waits for them, and re-layouts  1.49 us

profile of v3, /device:TPU:1, one launch (start us, length us, event | category | flops | bytes accessed | tf_op | source)
XLA Modules:
  0.0 55.8 jit_solution(560113684028332080)
XLA Ops:
  1.9 52.4 %purify.1 = (bf16[3,256,256]{2,1,0:T(8,128)(2,1)S(1)}, bf16[3,256,256]{2,1,0:T(8,128)(2,1)S(1)}) custom-call(bf16[3,256,256]{2,1,0:T(8,128)(2,1)} %bitcast.12, bf16[3,256,256]{2,1,0:T(8,128)(2,1)} %bitcast.13, s32[3]{0:T(128)} %bitcast.14, s32[3]{0:T(128)} %bitcast.15, s32[1]{0:T(128)} %bitcast.8.count_a_hbm, s32[1]{0:T(128)} %bitcast.9.count_b_hbm), custom_call_target="tpu_custom_call" | custom-call | tf_op jit(solution)/shard_map/purify/pallas_call | solution.py:423
  54.3 0.7 %copy.10 = bf16[1,1,1,3,256,256]{5,4,3,2,1,0:T(8,128)(2,1)} copy(bf16[1,1,1,3,256,256]{5,4,3,2,1,0:T(8,128)(2,1)S(1)} %bitcast.11) | data formatting | bytes 786432
  55.1 0.7 %copy.11 = bf16[1,1,1,3,256,256]{5,4,3,2,1,0:T(8,128)(2,1)} copy(bf16[1,1,1,3,256,256]{5,4,3,2,1,0:T(8,128)(2,1)S(1)} %bitcast.10) | data formatting | bytes 786432

commit v4 on v3

--- a/solution.py
+++ b/solution.py
@@ -60,7 +60,7 @@
     dens_a, dens_b, codes_a_hbm, codes_b_hbm, count_a_hbm, count_b_hbm, out_a, out_b,
     codes_a, codes_b, count_a, count_b, loaded, swap_out, swap_in, meta_out, meta_in, up, up_late, down, down_late,
     held_00, held_01, held_10, held_11, fresh_00, fresh_01, fresh_10, fresh_11, back,
-    load_sem, swap_send, swap_recv, meta_sem, halo_send, halo_recv, back_send, back_recv, via_send, via_recv,
+    load_sem, swap_send, swap_recv, meta_sem, halo_send, halo_recv, back_send, back_recv, via_send, via_recv, turn,
 ):
     held = ((held_00, held_01), (held_10, held_11))
     fresh = ((fresh_00, fresh_01), (fresh_10, fresh_11))
@@ -203,7 +203,7 @@
             return [(None, whole)]
         if step == 0:
             other = [down_first, up_first][region](which)
-            cut = first_plane if region == 0 else last_plane & own[1]
+            cut = first_plane if region == 0 else last_plane if which == 0 else last_plane & own[1]
             return [(cut, other), (jnp.logical_not(cut), whole)]
         if which == 0:
             return [(None, whole)]
@@ -241,20 +241,42 @@
     pl.when(first_plane)(lambda: greet(relay_for))
     pl.when(last_plane)(lambda: greet(relay_of))
     meta.start()
+    at_jump = first_plane | last_plane
+    edge_row = jnp.where(last_plane, 1, 0)
+
+    def own_halos(region, which):
+        send(0, region, OUT_X, which)
+        send(0, region, OUT_Z, which)
+
+    def own_inner(region):
+        for name in (IN_X, IN_Z):
+            for which in (0, 1):
+                send(0, region, name, which)
+
     for region in (0, 1):
 
-        @pl.when(own[region])
+        @pl.when(own[region] & jnp.logical_not(at_jump & (edge_row != region)))
         def _():
             swap(0).start()
-            send(0, region, OUT_X, 0)
-            send(0, region, OUT_Z, 0)
+            own_halos(region, 0)
             swap(1).start()
-            send(0, region, OUT_X, 1)
-            send(0, region, OUT_Z, 1)
+            own_halos(region, 1)
             swap(2).start()
-            for name in (IN_X, IN_Z):
-                for which in (0, 1):
-                    send(0, region, name, which)
+            own_inner(region)
+
+        @pl.when(own[region] & at_jump & (edge_row != region))
+        def _():
+            own_halos(region, 0)
+            own_halos(region, 1)
+            own_inner(region)
+            pl.semaphore_wait(turn, 1)
+            for index in range(SLOTS):
+                swap(index).start()
+
+    @pl.when(at_jump & (core == edge_row))
+    def _():
+        swap(1).wait_send()
+        pl.semaphore_signal(turn, 1, device_id=(sibling, col), device_id_type=MESH)
 
     meta.wait_recv()
     order_other = [meta_in[index] for index in range(SLOTS)]
@@ -343,11 +365,15 @@
     def give_back(region, index):
         pl.when(jnp.logical_not(own[region]))(returned(region, index).start)
 
+    @pl.when(first_plane)
+    def _():
+        up_first(0).wait_recv()
+        up_first_on(0).start()
+
     @pl.when(first_plane & own[0])
     def _():
-        for which in (0, 1):
-            up_first(which).wait_recv()
-            up_first_on(which).start()
+        up_first(1).wait_recv()
+        up_first_on(1).start()
 
     arrived(0, 1)
     purify(0, 1, lambda index: None)
@@ -393,7 +419,10 @@
 
     meta.wait_send()
     for index in range(SLOTS):
-        swap(index).wait_send()
+        if index == 1:
+            pl.when(jnp.logical_not(at_jump & (core == edge_row)))(swap(index).wait_send)
+        else:
+            swap(index).wait_send()
         returned(0, index).wait_send()
     for step in (0, 1):
         for region in (0, 1):
@@ -410,9 +439,10 @@
     @pl.when(first_plane)
     def _():
         up_second_on().wait_send()
+        up_first_on(0).wait_send()
+        pl.when(own[0])(up_first_on(1).wait_send)
         for which in (0, 1):
             down_first_on(which).wait_send()
-            pl.when(own[0])(up_first_on(which).wait_send)
 
 
 def per_device(dens_a, dens_b, codes_a, codes_b, counts_a, counts_b):
@@ -451,6 +481,7 @@
             pltpu.SemaphoreType.DMA((SLOTS,)),
             pltpu.SemaphoreType.DMA((7,)),
             pltpu.SemaphoreType.DMA((6,)),
+            pltpu.SemaphoreType.REGULAR,
         ],
         compiler_params=pltpu.CompilerParams(
             collective_id=0, has_side_effects=True, vmem_limit_bytes=60 * 2**20

time: 56.6 us -> 55.3 us (0.977)
  Pallas kernels: 52.4 us -> 51.6 us
    pallas_call x1, Pallas kernels: 52.4 us -> 51.6 us  [per_device(): pl.pallas_call(kernel, out_shape=[pltpu.VMEM(stored, jnp.bfloat16)] * 2,...]
where the time goes in v4:
time: 55.3 us; the launch traced here: 55 us
  Pallas kernels  51.6 us (93%)
  between operations  1.93 us (3%)
  local copies, waits for them, and re-layouts  1.49 us (3%)
    pallas_call x1, Pallas kernels, per_device(): pl.pallas_call(kernel, out_shape=[pltpu.VMEM(stored, jnp.bfloat16)] * 2,...  51.6 us
    unnamed x2, local copies, waits for them, and re-layouts  1.49 us

profile of v4, /device:TPU:1, one launch (start us, length us, event | category | flops | bytes accessed | tf_op | source)
XLA Modules:
  0.0 55.0 jit_solution(115536230296423824)
XLA Ops:
  1.9 51.6 %purify.1 = (bf16[3,256,256]{2,1,0:T(8,128)(2,1)S(1)}, bf16[3,256,256]{2,1,0:T(8,128)(2,1)S(1)}) custom-call(bf16[3,256,256]{2,1,0:T(8,128)(2,1)} %bitcast.12, bf16[3,256,256]{2,1,0:T(8,128)(2,1)} %bitcast.13, s32[3]{0:T(128)} %bitcast.14, s32[3]{0:T(128)} %bitcast.15, s32[1]{0:T(128)} %bitcast.8.count_a_hbm, s32[1]{0:T(128)} %bitcast.9.count_b_hbm), custom_call_target="tpu_custom_call" | custom-call | tf_op jit(solution)/shard_map/purify/pallas_call | solution.py:453
  53.5 0.7 %copy.10 = bf16[1,1,1,3,256,256]{5,4,3,2,1,0:T(8,128)(2,1)} copy(bf16[1,1,1,3,256,256]{5,4,3,2,1,0:T(8,128)(2,1)S(1)} %bitcast.11) | data formatting | bytes 786432
  54.3 0.7 %copy.11 = bf16[1,1,1,3,256,256]{5,4,3,2,1,0:T(8,128)(2,1)} copy(bf16[1,1,1,3,256,256]{5,4,3,2,1,0:T(8,128)(2,1)S(1)} %bitcast.10) | data formatting | bytes 786432

commit v5 on v4

--- a/solution.py
+++ b/solution.py
@@ -58,7 +58,7 @@
 
 def kernel(
     dens_a, dens_b, codes_a_hbm, codes_b_hbm, count_a_hbm, count_b_hbm, out_a, out_b,
-    codes_a, codes_b, count_a, count_b, loaded, swap_out, swap_in, meta_out, meta_in, up, up_late, down, down_late,
+    codes_a, codes_b, count_a, count_b, loaded, swap_out, swap_in, meta_out, meta_in, up, up_late, down, down_late, down_mid,
     held_00, held_01, held_10, held_11, fresh_00, fresh_01, fresh_10, fresh_11, back,
     load_sem, swap_send, swap_recv, meta_sem, halo_send, halo_recv, back_send, back_recv, via_send, via_recv, turn,
 ):
@@ -197,12 +197,22 @@
         landing = held[1][1].at[beside(OUT_Z) + 1]
         return remote(down_late, landing, via_send.at[6], halo_recv.at[1, 1, OUT_Z], behind)
 
+    def down_own():
+        source = held[0][0].at[OUT_Z]
+        return remote(source, down_mid, halo_send.at[0, 0, OUT_Z, 1], via_recv.at[6], relay_for)
+
+    def down_own_on():
+        landing = held[0][1].at[beside(OUT_Z) + 1]
+        return remote(down_mid, landing, via_send.at[7], halo_recv.at[0, 1, OUT_Z], behind)
+
     def parts(step, region, name, which):
         whole = halo(step, region, name, which)
         if name != OUT_Z:
             return [(None, whole)]
         if step == 0:
             other = [down_first, up_first][region](which)
+            if region == 0 and which == 1:
+                return [(first_plane & own[1], other), (jnp.logical_not(first_plane), whole)]
             cut = first_plane if region == 0 else last_plane if which == 0 else last_plane & own[1]
             return [(cut, other), (jnp.logical_not(cut), whole)]
         if which == 0:
@@ -304,9 +314,19 @@
     @pl.when(first_plane)
     def _():
         pl.semaphore_wait(barrier, 2)
-        for which in (0, 1):
-            down_first(which).wait_recv()
-            down_first_on(which).start()
+        pl.when(own[0])(down_own().start)
+        down_first(0).wait_recv()
+        down_first_on(0).start()
+
+    @pl.when(first_plane & own[1])
+    def _():
+        down_first(1).wait_recv()
+        down_first_on(1).start()
+
+    @pl.when(last_plane & own[1])
+    def _():
+        down_own().wait_recv()
+        down_own_on().start()
 
     mine_first, mine_has = diagonal_first(order_mine)
     other_first, other_has = diagonal_first(order_other)
@@ -393,9 +413,13 @@
         down_second().wait_recv()
         down_second_on().start()
 
-    for region in (1, 0):
+    def finish(region):
         arrived(1, region)
         purify(1, region, functools.partial(give_back, region))
+
+    pl.when(last_plane)(lambda: finish(0))
+    finish(1)
+    pl.when(jnp.logical_not(last_plane))(lambda: finish(0))
 
     def write(out, names, order, source):
         for slot in range(SLOTS):
@@ -441,8 +465,11 @@
         up_second_on().wait_send()
         up_first_on(0).wait_send()
         pl.when(own[0])(up_first_on(1).wait_send)
-        for which in (0, 1):
-            down_first_on(which).wait_send()
+        down_first_on(0).wait_send()
+        pl.when(own[0])(down_own().wait_send)
+        pl.when(own[1])(down_first_on(1).wait_send)
+
+    pl.when(last_plane & own[1])(down_own_on().wait_send)
 
 
 def per_device(dens_a, dens_b, codes_a, codes_b, counts_a, counts_b):
@@ -469,6 +496,7 @@
             pltpu.VMEM((RELAYED, EDGE), jnp.bfloat16),
             pltpu.VMEM((2, EDGE, EDGE), jnp.bfloat16),
             pltpu.VMEM((EDGE, EDGE), jnp.bfloat16),
+            pltpu.VMEM((EDGE, EDGE), jnp.bfloat16),
             *[pltpu.VMEM((HELD, EDGE, EDGE), jnp.bfloat16)] * 4,
             *[pltpu.VMEM((SLOTS + 1, EDGE, EDGE), jnp.bfloat16)] * 5,
             pltpu.SemaphoreType.DMA((6,)),
@@ -479,8 +507,8 @@
             pltpu.SemaphoreType.DMA((2, 2, NONE)),
             pltpu.SemaphoreType.DMA((SLOTS,)),
             pltpu.SemaphoreType.DMA((SLOTS,)),
+            pltpu.SemaphoreType.DMA((8,)),
             pltpu.SemaphoreType.DMA((7,)),
-            pltpu.SemaphoreType.DMA((6,)),
             pltpu.SemaphoreType.REGULAR,
         ],
         compiler_params=pltpu.CompilerParams(

time: 55.3 us -> 52.4 us (0.948)
  the two profiles are of different devices: /device:TPU:1 before, /device:TPU:13 now
where the time goes in v5:
time: 52.4 us; the launch traced here: 52.3 us
  Pallas kernels  48.8 us (93%)
  between operations  1.93 us (4%)
  local copies, waits for them, and re-layouts  1.49 us (3%)
    pallas_call x1, Pallas kernels, per_device(): pl.pallas_call(kernel, out_shape=[pltpu.VMEM(stored, jnp.bfloat16)] * 2,...  48.8 us
    unnamed x2, local copies, waits for them, and re-layouts  1.49 us

profile of v5, /device:TPU:13, one launch (start us, length us, event | category | flops | bytes accessed | tf_op | source)
XLA Modules:
  0.0 52.3 jit_solution(9786181140518963839)
XLA Ops:
  1.9 48.8 %purify.1 = (bf16[3,256,256]{2,1,0:T(8,128)(2,1)S(1)}, bf16[3,256,256]{2,1,0:T(8,128)(2,1)S(1)}) custom-call(bf16[3,256,256]{2,1,0:T(8,128)(2,1)} %bitcast.12, bf16[3,256,256]{2,1,0:T(8,128)(2,1)} %bitcast.13, s32[3]{0:T(128)} %bitcast.14, s32[3]{0:T(128)} %bitcast.15, s32[1]{0:T(128)} %bitcast.8.count_a_hbm, s32[1]{0:T(128)} %bitcast.9.count_b_hbm), custom_call_target="tpu_custom_call" | custom-call | tf_op jit(solution)/shard_map/purify/pallas_call | solution.py:480
  50.8 0.7 %copy.10 = bf16[1,1,1,3,256,256]{5,4,3,2,1,0:T(8,128)(2,1)} copy(bf16[1,1,1,3,256,256]{5,4,3,2,1,0:T(8,128)(2,1)S(1)} %bitcast.11) | data formatting | bytes 786432
  51.5 0.7 %copy.11 = bf16[1,1,1,3,256,256]{5,4,3,2,1,0:T(8,128)(2,1)} copy(bf16[1,1,1,3,256,256]{5,4,3,2,1,0:T(8,128)(2,1)S(1)} %bitcast.10) | data formatting | bytes 786432

commit v6 on v5

--- a/solution.py
+++ b/solution.py
@@ -13,7 +13,7 @@
 EDGE = 256
 SLOTS = 3
 HELD = 16
-RELAYED = 192
+RELAYED = 128
 
 
 def beside(name):

time: 52.4 us -> 51.5 us (0.983)
  the two profiles are of different devices: /device:TPU:13 before, /device:TPU:16 now
where the time goes in v6:
time: 51.5 us; the launch traced here: 51.4 us
  Pallas kernels  47.9 us (93%)
  between operations  1.93 us (4%)
  local copies, waits for them, and re-layouts  1.49 us (3%)
    pallas_call x1, Pallas kernels, per_device(): pl.pallas_call(kernel, out_shape=[pltpu.VMEM(stored, jnp.bfloat16)] * 2,...  47.9 us
    unnamed x2, local copies, waits for them, and re-layouts  1.49 us

profile of v6, /device:TPU:16, one launch (start us, length us, event | category | flops | bytes accessed | tf_op | source)
XLA Modules:
  0.0 51.4 jit_solution(8687072303230471811)
XLA Ops:
  1.9 47.9 %purify.1 = (bf16[3,256,256]{2,1,0:T(8,128)(2,1)S(1)}, bf16[3,256,256]{2,1,0:T(8,128)(2,1)S(1)}) custom-call(bf16[3,256,256]{2,1,0:T(8,128)(2,1)} %bitcast.12, bf16[3,256,256]{2,1,0:T(8,128)(2,1)} %bitcast.13, s32[3]{0:T(128)} %bitcast.14, s32[3]{0:T(128)} %bitcast.15, s32[1]{0:T(128)} %bitcast.8.count_a_hbm, s32[1]{0:T(128)} %bitcast.9.count_b_hbm), custom_call_target="tpu_custom_call" | custom-call | tf_op jit(solution)/shard_map/purify/pallas_call | solution.py:480
  49.9 0.7 %copy.10 = bf16[1,1,1,3,256,256]{5,4,3,2,1,0:T(8,128)(2,1)} copy(bf16[1,1,1,3,256,256]{5,4,3,2,1,0:T(8,128)(2,1)S(1)} %bitcast.11) | data formatting | bytes 786432
  50.6 0.7 %copy.11 = bf16[1,1,1,3,256,256]{5,4,3,2,1,0:T(8,128)(2,1)} copy(bf16[1,1,1,3,256,256]{5,4,3,2,1,0:T(8,128)(2,1)S(1)} %bitcast.10) | data formatting | bytes 786432

commit v7 on v6

--- a/solution.py
+++ b/solution.py
@@ -375,7 +375,7 @@
     def spread(region):
         for name in range(NONE):
             held[1][region][name] = fresh[0][region][place(layout[region][0], name)]
-        for which in (0, 1):
+        for which in (1, 0) if region else (0, 1):
             for name in (OUT_Z, OUT_X) if region else (OUT_X, OUT_Z):
                 send(1, region, name, which)
         for name in (IN_X, IN_Z):

time: 51.5 us -> 51.5 us (level)
  no operation moved by 1% of the time
where the time goes in v7:
time: 51.5 us; the launch traced here: 51.4 us
  Pallas kernels  48 us (93%)
  between operations  1.93 us (4%)
  local copies, waits for them, and re-layouts  1.49 us (3%)
    pallas_call x1, Pallas kernels, per_device(): pl.pallas_call(kernel, out_shape=[pltpu.VMEM(stored, jnp.bfloat16)] * 2,...  48 us
    unnamed x2, local copies, waits for them, and re-layouts  1.49 us

profile of v7, /device:TPU:16, one launch (start us, length us, event | category | flops | bytes accessed | tf_op | source)
XLA Modules:
  0.0 51.4 jit_solution(12039694706126023371)
XLA Ops:
  1.9 48.0 %purify.1 = (bf16[3,256,256]{2,1,0:T(8,128)(2,1)S(1)}, bf16[3,256,256]{2,1,0:T(8,128)(2,1)S(1)}) custom-call(bf16[3,256,256]{2,1,0:T(8,128)(2,1)} %bitcast.12, bf16[3,256,256]{2,1,0:T(8,128)(2,1)} %bitcast.13, s32[3]{0:T(128)} %bitcast.14, s32[3]{0:T(128)} %bitcast.15, s32[1]{0:T(128)} %bitcast.8.count_a_hbm, s32[1]{0:T(128)} %bitcast.9.count_b_hbm), custom_call_target="tpu_custom_call" | custom-call | tf_op jit(solution)/shard_map/purify/pallas_call | solution.py:480
  49.9 0.7 %copy.10 = bf16[1,1,1,3,256,256]{5,4,3,2,1,0:T(8,128)(2,1)} copy(bf16[1,1,1,3,256,256]{5,4,3,2,1,0:T(8,128)(2,1)S(1)} %bitcast.11) | data formatting | bytes 786432
  50.6 0.7 %copy.11 = bf16[1,1,1,3,256,256]{5,4,3,2,1,0:T(8,128)(2,1)} copy(bf16[1,1,1,3,256,256]{5,4,3,2,1,0:T(8,128)(2,1)S(1)} %bitcast.10) | data formatting | bytes 786432
